TPU v7x, 32 devices: a whole 2x2x4 slice. The times are simulated.
32 devices in a mesh: fsdp: 4 (over y, x), ctx: 8 (over z, core).
Axes of the slice: x: 2, y: 2, z: 4, core: 2. Of those that a mesh axis runs over, the one named last changes fastest.
Arguments:
- tokens: bfloat16 [4, 8, 2, 64, 768], P('fsdp', 'ctx'), may hold values from -6 to 6
- cotangent: bfloat16 [4, 8, 2, 64, 768], P('fsdp', 'ctx'), may hold values from -6 to 6
- pair_of_rank: int32 [8], replicated, may hold values from 0 to 7, each once
- ln1_gain: bfloat16 [768], P('fsdp'), may hold values from 0.5 to 1.5
- ln1_shift: bfloat16 [768], P('fsdp'), may hold values from -4 to 4
- w_qkv: bfloat16 [768, 2304], P('fsdp'), may hold values from -0.21875 to 0.21875
- bias_q: bfloat16 [768], P('fsdp'), may hold values from -4 to 4
- bias_v: bfloat16 [768], P('fsdp'), may hold values from -4 to 4
- w_out: bfloat16 [768, 768], P('fsdp'), may hold values from -4 to 4
- bias_out: bfloat16 [768], P('fsdp'), may hold values from -4 to 4
- ln2_gain: bfloat16 [768], P('fsdp'), may hold values from 0.5 to 1.5
- ln2_shift: bfloat16 [768], P('fsdp'), may hold values from -4 to 4
- w_up: bfloat16 [768, 3072], P('fsdp'), may hold values from -0.21875 to 0.21875
- bias_up: bfloat16 [3072], P('fsdp'), may hold values from -4 to 4
- w_down: bfloat16 [3072, 768], P('fsdp'), may hold values from -0.109375 to 0.109375
- bias_down: bfloat16 [768], P('fsdp'), may hold values from -4 to 4
Outputs:
- layer_out: bfloat16 [4, 8, 2, 64, 768], P('fsdp', 'ctx')
- grad_tokens: bfloat16 [4, 8, 2, 64, 768], P('fsdp', 'ctx')
- grad_ln1_gain: float32 [768], P('fsdp')
- grad_ln1_shift: float32 [768], P('fsdp')
- grad_w_qkv: float32 [768, 2304], P('fsdp')
- grad_bias_q: float32 [768], P('fsdp')
- grad_bias_v: float32 [768], P('fsdp')
- grad_w_out: float32 [768, 768], P('fsdp')
- grad_bias_out: float32 [768], P('fsdp')
- grad_ln2_gain: float32 [768], P('fsdp')
- grad_ln2_shift: float32 [768], P('fsdp')
- grad_w_up: float32 [768, 3072], P('fsdp')
- grad_bias_up: float32 [3072], P('fsdp')
- grad_w_down: float32 [3072, 768], P('fsdp')
- grad_bias_down: float32 [768], P('fsdp')
Inputs may be any that keep to these rules, and one draw needn't show every extreme that they name: `pair_of_rank`: each of 0 to 7 once.
All inputs are finite; a program needn't handle non-finite values.
Results may differ from a plain program's by a relative error of at most 0.018.
Values may be sent and summed in bfloat16 or wider, within the bound.
A program may use at most 128 MiB of HBM per device.

v0:
```python
import jax
import jax.numpy as jnp
from jax import lax
from jax.sharding import PartitionSpec as P

HDIM = 64


EPS = 1e-05
MASKED = -1e30


def norm_rows(z, gain, shift):
    mean = jnp.mean(z, axis=-1, keepdims=True)
    cent = z - mean
    var = jnp.mean(cent * cent, axis=-1, keepdims=True)
    return cent * lax.rsqrt(var + EPS) * gain + shift


def body(
    tokens,
    cotangent,
    pair_of_rank,
    ln1_gain,
    ln1_shift,
    w_qkv,
    bias_q,
    bias_v,
    w_out,
    bias_out,
    ln2_gain,
    ln2_shift,
    w_up,
    bias_up,
    w_down,
    bias_down,
):
    seqs = tokens.shape[0]
    blk = tokens.shape[3]
    width = tokens.shape[4]
    parts = lax.axis_size("ctx")
    rank = lax.axis_index("ctx")
    local = 2 * blk
    rows = seqs * local
    span = parts * local
    heads = width // HDIM
    scale = HDIM ** (-0.5)
    attn_params = (
        lax.all_gather(ln1_gain, "fsdp", axis=0, tiled=True),
        lax.all_gather(ln1_shift, "fsdp", axis=0, tiled=True),
        lax.all_gather(w_qkv, "fsdp", axis=0, tiled=True),
        lax.all_gather(bias_q, "fsdp", axis=0, tiled=True),
        lax.all_gather(bias_v, "fsdp", axis=0, tiled=True),
        lax.all_gather(w_out, "fsdp", axis=0, tiled=True),
        lax.all_gather(bias_out, "fsdp", axis=0, tiled=True),
    )
    gain1, shift1, wqkv_all, bq_all, bv_all, wout_all, bout_all = attn_params
    gain1 = gain1.astype(jnp.float32)
    shift1 = shift1.astype(jnp.float32)
    inputs = tokens.reshape(rows, width).astype(jnp.float32)
    a_one = norm_rows(inputs, gain1, shift1).astype(jnp.bfloat16)
    qkv_bias = jnp.concatenate(
        [bq_all.astype(jnp.float32), jnp.zeros((width,), jnp.float32), bv_all.astype(jnp.float32)]
    )
    qkv = (jnp.dot(a_one, wqkv_all, preferred_element_type=jnp.float32) + qkv_bias).astype(
        jnp.bfloat16
    )
    query = qkv[:, :width].reshape(seqs, local, width)
    keys = qkv[:, width : 2 * width].reshape(seqs, 1, 2, blk, width)
    values = qkv[:, 2 * width :].reshape(seqs, 1, 2, blk, width)
    keys_all, values_all = (
        lax.all_gather(keys, "ctx", axis=1, tiled=True),
        lax.all_gather(values, "ctx", axis=1, tiled=True),
    )
    keys_all = keys_all.reshape(seqs, span, width)
    values_all = values_all.reshape(seqs, span, width)
    own = pair_of_rank[rank]
    offsets = jnp.arange(blk, dtype=jnp.int32)
    query_pos = jnp.concatenate([own * blk + offsets, (2 * parts - 1 - own) * blk + offsets])
    key_blocks = jnp.stack([pair_of_rank, 2 * parts - 1 - pair_of_rank], axis=1)
    key_pos = (key_blocks[:, :, None] * blk + offsets[None, None, :]).reshape(span)
    visible = query_pos[:, None] >= key_pos[None, :]
    indices = jnp.arange(seqs * heads, dtype=jnp.int32)

    def head_slices(index):
        seq = index // heads
        col = index % heads * HDIM
        qpart = lax.dynamic_slice(query, (seq, 0, col), (1, local, HDIM))[0]
        kpart = lax.dynamic_slice(keys_all, (seq, 0, col), (1, span, HDIM))[0]
        vpart = lax.dynamic_slice(values_all, (seq, 0, col), (1, span, HDIM))[0]
        return (qpart, kpart, vpart)

    def scores_of(qpart, kpart):
        raw = (
            lax.dot_general(
                qpart, kpart, (((1,), (1,)), ((), ())), preferred_element_type=jnp.float32
            )
            * scale
        )
        return jnp.where(visible, raw, MASKED)

    def forward_head(index):
        qpart, kpart, vpart = head_slices(index)
        scores = scores_of(qpart, kpart)
        top = jnp.max(scores, axis=1, keepdims=True)
        expo = jnp.exp(scores - top)
        total = jnp.sum(expo, axis=1, keepdims=True)
        probs = (expo / total).astype(jnp.bfloat16)
        result = jnp.dot(probs, vpart, preferred_element_type=jnp.float32)
        return (result, (top + jnp.log(total))[:, 0])

    head_outs, log_totals = lax.map(forward_head, indices)
    mixed = (
        head_outs.reshape(seqs, heads, local, HDIM)
        .transpose(0, 2, 1, 3)
        .reshape(rows, width)
        .astype(jnp.bfloat16)
    )
    branch = jnp.dot(mixed, wout_all, preferred_element_type=jnp.float32) + bout_all.astype(
        jnp.float32
    )
    resid = inputs + branch
    mlp_params = (
        lax.all_gather(ln2_gain, "fsdp", axis=0, tiled=True),
        lax.all_gather(ln2_shift, "fsdp", axis=0, tiled=True),
        lax.all_gather(w_up, "fsdp", axis=0, tiled=True),
        lax.all_gather(bias_up, "fsdp", axis=0, tiled=True),
        lax.all_gather(w_down, "fsdp", axis=0, tiled=True),
        lax.all_gather(bias_down, "fsdp", axis=0, tiled=True),
    )
    gain2, shift2, wup_all, bup_all, wdown_all, bdown_all = mlp_params
    gain2 = gain2.astype(jnp.float32)
    shift2 = shift2.astype(jnp.float32)
    a_two = norm_rows(resid, gain2, shift2).astype(jnp.bfloat16)
    upper = jnp.dot(a_two, wup_all, preferred_element_type=jnp.float32) + bup_all.astype(
        jnp.float32
    )
    active, gelu_pull = jax.vjp(jax.nn.gelu, upper)
    a_three = active.astype(jnp.bfloat16)
    result_rows = (
        resid
        + jnp.dot(a_three, wdown_all, preferred_element_type=jnp.float32)
        + bdown_all.astype(jnp.float32)
    )
    layer_out = result_rows.astype(jnp.bfloat16).reshape(tokens.shape)
    grad_rows = cotangent.reshape(rows, width).astype(jnp.float32)
    d_mlp = grad_rows.astype(jnp.bfloat16)
    g_bdown = jnp.sum(d_mlp.astype(jnp.float32), axis=0)
    g_wdown = lax.dot_general(
        a_three, d_mlp, (((0,), (0,)), ((), ())), preferred_element_type=jnp.float32
    )
    d_active = lax.dot_general(
        d_mlp, wdown_all, (((1,), (1,)), ((), ())), preferred_element_type=jnp.float32
    )
    d_upper = gelu_pull(d_active)[0].astype(jnp.bfloat16)
    g_bup = jnp.sum(d_upper.astype(jnp.float32), axis=0)
    g_wup = lax.dot_general(
        a_two, d_upper, (((0,), (0,)), ((), ())), preferred_element_type=jnp.float32
    )
    d_htwo = lax.dot_general(
        d_upper, wup_all, (((1,), (1,)), ((), ())), preferred_element_type=jnp.float32
    )
    norm_two_pull = jax.vjp(norm_rows, resid, gain2, shift2)[1]
    d_resid_norm, g_gain2, g_shift2 = norm_two_pull(d_htwo)
    d_resid = grad_rows + d_resid_norm
    mlp_shards = (
        lax.psum_scatter(
            g_gain2.astype(jnp.bfloat16), "fsdp", scatter_dimension=0, tiled=True
        ).astype(jnp.float32),
        lax.psum_scatter(
            g_shift2.astype(jnp.bfloat16), "fsdp", scatter_dimension=0, tiled=True
        ).astype(jnp.float32),
        lax.psum_scatter(
            g_wup.astype(jnp.bfloat16), "fsdp", scatter_dimension=0, tiled=True
        ).astype(jnp.float32),
        lax.psum_scatter(
            g_bup.astype(jnp.bfloat16), "fsdp", scatter_dimension=0, tiled=True
        ).astype(jnp.float32),
        lax.psum_scatter(
            g_wdown.astype(jnp.bfloat16), "fsdp", scatter_dimension=0, tiled=True
        ).astype(jnp.float32),
        lax.psum_scatter(
            g_bdown.astype(jnp.bfloat16), "fsdp", scatter_dimension=0, tiled=True
        ).astype(jnp.float32),
    )
    mlp_done = (
        lax.psum(mlp_shards[0].astype(jnp.bfloat16), "ctx").astype(jnp.float32),
        lax.psum(mlp_shards[1].astype(jnp.bfloat16), "ctx").astype(jnp.float32),
        lax.psum(mlp_shards[2].astype(jnp.bfloat16), "ctx").astype(jnp.float32),
        lax.psum(mlp_shards[3].astype(jnp.bfloat16), "ctx").astype(jnp.float32),
        lax.psum(mlp_shards[4].astype(jnp.bfloat16), "ctx").astype(jnp.float32),
        lax.psum(mlp_shards[5].astype(jnp.bfloat16), "ctx").astype(jnp.float32),
    )
    d_branch = d_resid.astype(jnp.bfloat16)
    g_bout = jnp.sum(d_branch.astype(jnp.float32), axis=0)
    g_wout = lax.dot_general(
        mixed, d_branch, (((0,), (0,)), ((), ())), preferred_element_type=jnp.float32
    )
    d_mixed = lax.dot_general(
        d_branch, wout_all, (((1,), (1,)), ((), ())), preferred_element_type=jnp.float32
    )
    d_mixed = d_mixed.astype(jnp.bfloat16).reshape(seqs, local, width)

    def query_side(index):
        qpart, kpart, vpart = head_slices(index)
        seq = index // heads
        col = index % heads * HDIM
        d_out = lax.dynamic_slice(d_mixed, (seq, 0, col), (1, local, HDIM))[0]
        probs = jnp.exp(scores_of(qpart, kpart) - log_totals[index][:, None])
        d_probs = lax.dot_general(
            d_out, vpart, (((1,), (1,)), ((), ())), preferred_element_type=jnp.float32
        )
        delta = jnp.sum(probs * d_probs, axis=1, keepdims=True)
        d_scores = (probs * (d_probs - delta)).astype(jnp.bfloat16)
        d_query = jnp.dot(d_scores, kpart, preferred_element_type=jnp.float32) * scale
        return (qpart, d_out, probs, d_scores, d_query, delta[:, 0])

    def backward_head(index):
        qpart, d_out, probs, d_scores, d_query, delta = query_side(index)
        d_key = (
            lax.dot_general(
                d_scores, qpart, (((0,), (0,)), ((), ())), preferred_element_type=jnp.float32
            )
            * scale
        )
        d_value = lax.dot_general(
            probs.astype(jnp.bfloat16),
            d_out,
            (((0,), (0,)), ((), ())),
            preferred_element_type=jnp.float32,
        )
        return (d_query, d_key, d_value)

    dq_heads, dk_heads, dv_heads = lax.map(backward_head, indices)
    d_keys_all = (
        dk_heads.reshape(seqs, heads, span, HDIM)
        .transpose(0, 2, 1, 3)
        .reshape(seqs, parts, 2, blk, width)
    )
    d_values_all = (
        dv_heads.reshape(seqs, heads, span, HDIM)
        .transpose(0, 2, 1, 3)
        .reshape(seqs, parts, 2, blk, width)
    )
    d_keys_own, d_values_own = (
        lax.psum_scatter(d_keys_all, "ctx", scatter_dimension=1, tiled=True),
        lax.psum_scatter(d_values_all, "ctx", scatter_dimension=1, tiled=True),
    )
    d_keys_rows = d_keys_own.reshape(rows, width)
    d_values_rows = d_values_own.reshape(rows, width)
    d_query_rows = (
        dq_heads.reshape(seqs, heads, local, HDIM).transpose(0, 2, 1, 3).reshape(rows, width)
    )
    d_qkv = jnp.concatenate([d_query_rows, d_keys_rows, d_values_rows], axis=1).astype(jnp.bfloat16)
    g_bq = jnp.sum(d_qkv[:, :width].astype(jnp.float32), axis=0)
    g_bv = jnp.sum(d_qkv[:, 2 * width :].astype(jnp.float32), axis=0)
    g_wqkv = lax.dot_general(
        a_one, d_qkv, (((0,), (0,)), ((), ())), preferred_element_type=jnp.float32
    )
    d_hone = lax.dot_general(
        d_qkv, wqkv_all, (((1,), (1,)), ((), ())), preferred_element_type=jnp.float32
    )
    norm_one_pull = jax.vjp(norm_rows, inputs, gain1, shift1)[1]
    d_input_norm, g_gain1, g_shift1 = norm_one_pull(d_hone)
    grad_tokens = (d_resid + d_input_norm).astype(jnp.bfloat16).reshape(tokens.shape)
    attn_shards = (
        lax.psum_scatter(
            g_gain1.astype(jnp.bfloat16), "fsdp", scatter_dimension=0, tiled=True
        ).astype(jnp.float32),
        lax.psum_scatter(
            g_shift1.astype(jnp.bfloat16), "fsdp", scatter_dimension=0, tiled=True
        ).astype(jnp.float32),
        lax.psum_scatter(
            g_wqkv.astype(jnp.bfloat16), "fsdp", scatter_dimension=0, tiled=True
        ).astype(jnp.float32),
        lax.psum_scatter(g_bq.astype(jnp.bfloat16), "fsdp", scatter_dimension=0, tiled=True).astype(
            jnp.float32
        ),
        lax.psum_scatter(g_bv.astype(jnp.bfloat16), "fsdp", scatter_dimension=0, tiled=True).astype(
            jnp.float32
        ),
        lax.psum_scatter(
            g_wout.astype(jnp.bfloat16), "fsdp", scatter_dimension=0, tiled=True
        ).astype(jnp.float32),
        lax.psum_scatter(
            g_bout.astype(jnp.bfloat16), "fsdp", scatter_dimension=0, tiled=True
        ).astype(jnp.float32),
    )
    attn_done = (
        lax.psum(attn_shards[0].astype(jnp.bfloat16), "ctx").astype(jnp.float32),
        lax.psum(attn_shards[1].astype(jnp.bfloat16), "ctx").astype(jnp.float32),
        lax.psum(attn_shards[2].astype(jnp.bfloat16), "ctx").astype(jnp.float32),
        lax.psum(attn_shards[3].astype(jnp.bfloat16), "ctx").astype(jnp.float32),
        lax.psum(attn_shards[4].astype(jnp.bfloat16), "ctx").astype(jnp.float32),
        lax.psum(attn_shards[5].astype(jnp.bfloat16), "ctx").astype(jnp.float32),
        lax.psum(attn_shards[6].astype(jnp.bfloat16), "ctx").astype(jnp.float32),
    )
    finished = tuple(attn_done) + tuple(mlp_done)
    return (
        layer_out,
        grad_tokens,
        finished[0],
        finished[1],
        finished[2],
        finished[3],
        finished[4],
        finished[5],
        finished[6],
        finished[7],
        finished[8],
        finished[9],
        finished[10],
        finished[11],
        finished[12],
    )


def solution(mesh):
    in_specs = (
        P("fsdp", "ctx", None, None, None),
        P("fsdp", "ctx", None, None, None),
        P(),
        P("fsdp"),
        P("fsdp"),
        P("fsdp", None),
        P("fsdp"),
        P("fsdp"),
        P("fsdp", None),
        P("fsdp"),
        P("fsdp"),
        P("fsdp"),
        P("fsdp", None),
        P("fsdp"),
        P("fsdp", None),
        P("fsdp"),
    )
    out_specs = (
        P("fsdp", "ctx", None, None, None),
        P("fsdp", "ctx", None, None, None),
        P("fsdp"),
        P("fsdp"),
        P("fsdp", None),
        P("fsdp"),
        P("fsdp"),
        P("fsdp", None),
        P("fsdp"),
        P("fsdp"),
        P("fsdp"),
        P("fsdp", None),
        P("fsdp"),
        P("fsdp", None),
        P("fsdp"),
    )
    return jax.shard_map(body, mesh=mesh, in_specs=in_specs, out_specs=out_specs, check_vma=False)
```

profile of v0, /device:TPU:0, one launch (start us, length us, event | category | flops | bytes accessed | tf_op | source)
XLA Modules:
  0.0 830.6 jit_solution(892679151325658153)
XLA Ops:
  12.3 17.9 %all-reduce.20 = (bf16[768]{0:T(1024)(128)(2,1)S(1)}, bf16[768]{0:T(1024)(128)(2,1)S(1)}, bf16[768]{0:T(1024)(128)(2,1)S(1)}, bf16[768]{0:T(1024)(128)(2,1)S(1)}...) all-reduce(bf16[768]{0:T(1024)(128)(2,1)S(1)} %dynamic-update-slice, ...), channel_id=1, replica_groups=mesh['fsdp'=4,'ctx'=8] {'fsdp'}, use_global_device_ids=true, to_apply=%add.1 | all-reduce | flops 5376 | bytes 21504
  30.3 29.7 %all-gather.8.cloned.1.call-done = bf16[768,2304]{1,0:T(8,128)(2,1)} async-done(((bf16[192,2304]{1,0:T(8,128)(2,1)}), bf16[768,2304]{1,0:T(8,128)(2,1)}) %all-gather.8.cloned.1.call-update) | async-done | bytes 3538960 | tf_op jit(solution)/shard_map/all_gather | solution.py:51
  60.0 2.6 fusion.47
  67.5 8.4 %all-gather = bf16[4,1,768]{2,1,0:T(2,128)(2,1)S(1)} all-gather(bf16[1,1,768]{2,1,0:T(2,128)(2,1)S(1)} %reshape.296), channel_id=1, replica_groups=mesh['fsdp'=4,'ctx'=8] {'fsdp'}, dimensions={0}, use_global_device_ids=true | all-gather | bytes 7680 | tf_op jit(solution)/shard_map/all_gather | solution.py:127
  76.0 43.0 %all-gather.18.cloned.1.call-done = bf16[3072,768]{1,0:T(8,128)(2,1)} async-done(((bf16[768,768]{1,0:T(8,128)(2,1)}), bf16[3072,768]{1,0:T(8,128)(2,1)}) %all-gather.18.cloned.1.call-update) | async-done | bytes 4718608 | tf_op jit(solution)/shard_map/all_gather | solution.py:128
  119.0 5.1 fusion.76
  124.1 22.2 %all-gather.10.cloned.1.call-done = bf16[1,8,2,64,768]{4,3,2,0,1:T(8,128)(2,1)} async-done(((bf16[1,1,2,64,768]{4,3,2,0,1:T(8,128)(2,1)}), bf16[1,8,2,64,768]{4,3,2,0,1:T(8,128)(2,1)}) %all-gather.10.cloned.1.call-update) | async-done | bytes 1572880 | tf_op jit(solution)/shard_map/all_gather | solution.py:72
  146.3 26.7 %all-gather.12.cloned.1.call-done = bf16[1,8,2,64,768]{4,3,2,0,1:T(8,128)(2,1)} async-done(((bf16[1,1,2,64,768]{4,3,2,0,1:T(8,128)(2,1)}), bf16[1,8,2,64,768]{4,3,2,0,1:T(8,128)(2,1)}) %all-gather.12.cloned.1.call-update) | async-done | bytes 1572880 | tf_op jit(solution)/shard_map/all_gather | solution.py:73
  173.0 66.3 %while.32 = (s32[]{:T(128)}, bf16[12,128,64]{1,2,0:T(8,128)(2,1)S(1)}, f32[12,128]{1,0:T(8,128)}, s32[12]{0:T(128)S(1)}, bf16[1,128,768]{2,1,0:T(8,128)(2,1)S(1)...) while((s32[]{:T(128)}, ...), condition=%wide.region_5.6_spmd.clone, body=%wide.region_2.5_spmd.clone.sunk | while | flops 34733964 | bytes 2173717 | solution.py:112
  241.9 18.9 %all-gather.16.cloned.1.call-done = bf16[768,3072]{1,0:T(8,128)(2,1)} async-done(((bf16[192,3072]{1,0:T(8,128)(2,1)}), bf16[768,3072]{1,0:T(8,128)(2,1)}) %all-gather.16.cloned.1.call-update) | async-done | bytes 4718608 | tf_op jit(solution)/shard_map/all_gather | solution.py:126
  260.9 5.5 fusion.66
  273.5 153.6 %while.33 = (s32[]{:T(128)}, bf16[12,128,64]{1,2,0:T(8,128)(2,1)}, f32[12,1024,64]{1,2,0:T(8,128)}, f32[12,1024,64]{1,2,0:T(8,128)}, s32[12]{0:T(128)}, /*index=...) while((s32[]{:T(128)}, bf16[12,128,64]{1,2,0:T(8,128)(2,1)}, ...), condition=%wide.region_12.13_spmd.clone, body=%wide.region_10.12_spmd.clone.sunk | while | flops 85270416 | bytes 5416279 | solution.py:234
  427.1 7.5 reshape.264
  434.6 9.6 %copy.44 = f32[1,8,2,64,768]{4,3,2,0,1:T(8,128)} copy(f32[1,8,2,64,768]{3,2,1,4,0:T(2,128)} %reshape.264) | data formatting | bytes 6291456 | tf_op jit(solution)/shard_map/reshape | solution.py:238
  444.2 7.5 reshape.267
  451.7 9.6 %copy.46 = f32[1,8,2,64,768]{4,3,2,0,1:T(8,128)} copy(f32[1,8,2,64,768]{3,2,1,4,0:T(2,128)} %reshape.267) | data formatting | bytes 6291456 | tf_op jit(solution)/shard_map/reshape | solution.py:243
  461.3 2.5 convolution_convert_fusion.3
  464.1 3.8 convolution_convert_fusion
  468.5 4.4 convolution_convert_fusion.1
  473.0 11.7 %reduce-scatter.7.cloned.1.call-done = f32[1,1,2,64,768]{4,3,2,0,1:T(8,128)} async-done(((f32[1,8,2,64,768]{4,3,2,0,1:T(8,128)}), f32[1,1,2,64,768]{4,3,2,0,1:T(8,128)}) %reduce-scatter.7.cloned.1.call-update) | async-done | bytes 393232 | tf_op jit(solution)/shard_map/reduce_scatter | solution.py:246
  485.8 40.6 %reduce-scatter.9.cloned.1.call-done = f32[1,1,2,64,768]{4,3,2,0,1:T(8,128)} async-done(((f32[1,8,2,64,768]{4,3,2,0,1:T(8,128)}), f32[1,1,2,64,768]{4,3,2,0,1:T(8,128)}) %reduce-scatter.9.cloned.1.call-update) | async-done | bytes 393232 | tf_op jit(solution)/shard_map/reduce_scatter | solution.py:247
  528.9 3.9 convolution_convert_fusion.2
  534.9 22.7 %reduce-scatter.13.cloned.1.call-done = bf16[192,768]{1,0:T(8,128)(2,1)} async-done(((bf16[768,768]{1,0:T(8,128)(2,1)}), bf16[192,768]{1,0:T(8,128)(2,1)}) %reduce-scatter.13.cloned.1.call-update) | async-done | bytes 294928 | tf_op jit(solution)/shard_map/reduce_scatter | solution.py:282
  557.6 59.9 %reduce-scatter.17.cloned.1.call-done = bf16[768,768]{1,0:T(8,128)(2,1)} async-done(((bf16[3072,768]{1,0:T(8,128)(2,1)}), bf16[768,768]{1,0:T(8,128)(2,1)}) %reduce-scatter.17.cloned.1.call-update) | async-done | bytes 1179664 | tf_op jit(solution)/shard_map/reduce_scatter | solution.py:179
  617.5 60.1 %reduce-scatter.15.cloned.1.call-done = bf16[192,3072]{1,0:T(8,128)(2,1)} async-done(((bf16[768,3072]{1,0:T(8,128)(2,1)}), bf16[192,3072]{1,0:T(8,128)(2,1)}) %reduce-scatter.15.cloned.1.call-update) | async-done | bytes 1179664 | tf_op jit(solution)/shard_map/reduce_scatter | solution.py:173
  677.7 50.2 %reduce-scatter.11.cloned.1.call-done = bf16[192,2304]{1,0:T(8,128)(2,1)} async-done(((bf16[768,2304]{1,0:T(8,128)(2,1)}), bf16[192,2304]{1,0:T(8,128)(2,1)}) %reduce-scatter.11.cloned.1.call-update) | async-done | bytes 884752 | tf_op jit(solution)/shard_map/reduce_scatter | solution.py:273
  728.8 4.0 fusion.65
  733.1 16.0 %all-reduce.19 = (bf16[768]{0:T(1024)(128)(2,1)S(1)}, bf16[768]{0:T(1024)(128)(2,1)S(1)}, bf16[768]{0:T(1024)(128)(2,1)S(1)}, bf16[768]{0:T(1024)(128)(2,1)S(1)}...) all-reduce(bf16[768]{0:T(1024)(128)(2,1)} %copy-done.21, ...), channel_id=1, replica_groups=mesh['fsdp'=4,'ctx'=8] {'fsdp'}, use_global_device_ids=true, to_apply=%add.7 | all-reduce | flops 9984 | bytes 39936
  749.8 15.1 %all-reduce.17 = (bf16[192]{0:T(256)(128)(2,1)S(1)}, bf16[192]{0:T(256)(128)(2,1)S(1)}, bf16[192]{0:T(256)(128)(2,1)S(1)}, bf16[192]{0:T(256)(128)(2,1)S(1)}, bf...) all-reduce(bf16[192]{0:T(256)(128)(2,1)S(1)} %dynamic-slice.9, ...), channel_id=1, replica_groups=mesh['fsdp'=4,'ctx'=8] {'ctx'}, use_global_device_ids=true, to_apply=%region_19.20 | all-reduce | flops 2304 | bytes 9216 | tf_op jit(solution)/shard_map/psum | solution.py:290
  771.6 4.1 fusion.57
  775.7 40.7 %all-reduce.23.cloned.1.call-done = (bf16[192,2304]{1,0:T(8,128)(2,1)}, bf16[192,768]{1,0:T(8,128)(2,1)}, bf16[192,3072]{1,0:T(8,128)(2,1)}, bf16[768,768]{1,0:T(8,128)(2,1)}) async-done(((bf16[192,2304]{1,0:T(8,128)(2,1)}, bf16[192,768]{1,0:T(8,128)(2,1)}, bf16[192,3072]{1,0:T(8,128)(2,1)}, bf16[768,768]{1,0:T(8,128)(2,1)}), (bf16[192,2304]{1,0:T(8,128)(2,1)}, bf16[192,768]{1,0:T(8,128)(2,1)}, ...) | async-done | bytes 3538960 | tf_op jit(solution)/shard_map/psum | solution.py:292
  818.3 2.5 convert_element_type.229
  (370 shorter events, 217.1 us)
Async XLA Ops:
  7.2 4.3 copy-start.34
  7.3 4.5 copy-start.35
  7.3 4.8 copy-start.36
  7.3 52.7 %all-gather.8.cloned.1.call-start = ((), (), s32[]{:S(2)}) async-start(), calls=%async_computation.6 | async-start | bytes 4423680 | tf_op jit(solution)/shard_map/all_gather | solution.py:51
  8.0 110.9 %all-gather.18.cloned.1.call-start = ((), (), s32[]{:S(2)}) async-start(), calls=%async_computation.11 | async-start | bytes 5898240 | tf_op jit(solution)/shard_map/all_gather | solution.py:128
  8.8 137.5 %all-gather.10.cloned.1.call-start = ((), (), s32[]{:S(2)}) async-start(), calls=%async_computation.7 | async-start | bytes 1769472 | tf_op jit(solution)/shard_map/all_gather | solution.py:72
  9.0 51.0 %copy-start.22 = (f32[128]{0:T(128)}, f32[128]{0:T(128)S(1)}, u32[]{:S(2)}) copy-start(f32[128]{0:T(128)S(1)} %div.61) | copy-start | bytes 1540
  9.3 50.7 %copy-start.24 = (f32[128]{0:T(128)}, f32[128]{0:T(128)S(1)}, u32[]{:S(2)}) copy-start(f32[128]{0:T(128)S(1)} %rsqrt.22) | copy-start | bytes 1540
  30.3 29.7 %copy-start.4 = (bf16[128,768]{1,0:T(8,128)(2,1)}, bf16[128,768]{1,0:T(8,128)(2,1)S(1)}, u32[]{:S(2)}) copy-start(bf16[128,768]{1,0:T(8,128)(2,1)S(1)} %add_convert_fusion.2) | copy-start | bytes 589828
  62.7 4.7 copy-start.28
  62.7 56.3 %copy-start.1 = (bf16[1,1,2,64,768]{4,3,2,1,0:T(8,128)(2,1)S(1)}, bf16[1,1,2,64,768]{4,3,2,1,0:T(8,128)(2,1)}, u32[]{:S(2)}) copy-start(bf16[1,1,2,64,768]{4,3,2,1,0:T(8,128)(2,1)} %param.21) | copy-start | bytes 589828
  63.5 109.4 %all-gather.12.cloned.1.call-start = ((), (), s32[]{:S(2)}) async-start(), calls=%async_computation.8 | async-start | bytes 1769472 | tf_op jit(solution)/shard_map/all_gather | solution.py:73
  64.1 175.2 %all-gather.14.cloned.1.call-start = ((), (), s32[]{:S(2)}) async-start(), calls=%async_computation.9 | async-start | bytes 1474560 | tf_op jit(solution)/shard_map/all_gather | solution.py:54
  64.7 196.2 %all-gather.16.cloned.1.call-start = ((), (), s32[]{:S(2)}) async-start(), calls=%async_computation.10 | async-start | bytes 5898240 | tf_op jit(solution)/shard_map/all_gather | solution.py:126
  65.3 419.4 %reduce-scatter.7.cloned.1.call-start = ((), (), s32[]{:S(2)}) async-start(), calls=%async_computation.12 | async-start | bytes 3538944 | tf_op jit(solution)/shard_map/reduce_scatter | solution.py:246
  239.3 21.6 %copy-start.7 = (bf16[12,128,64]{1,2,0:T(8,128)(2,1)}, bf16[12,128,64]{1,2,0:T(8,128)(2,1)S(1)}, u32[]{:S(2)}) copy-start(bf16[12,128,64]{1,2,0:T(8,128)(2,1)S(1)} %get-tuple-element.258) | copy-start | bytes 589828
  241.7 24.7 %copy-start.15 = (f32[128]{0:T(128)}, f32[128]{0:T(128)S(1)}, u32[]{:S(2)}) copy-start(f32[128]{0:T(128)S(1)} %broadcast_multiply_fusion.1) | copy-start | bytes 1540
  241.9 24.5 %copy-start.17 = (f32[128]{0:T(128)}, f32[128]{0:T(128)S(1)}, u32[]{:S(2)}) copy-start(f32[128]{0:T(128)S(1)} %fusion.61) | copy-start | bytes 1540
  260.9 5.5 copy-start.3
  444.2 82.2 %reduce-scatter.9.cloned.1.call-start = ((), (), s32[]{:S(2)}) async-start(), calls=%async_computation.13 | async-start | bytes 3538944 | tf_op jit(solution)/shard_map/reduce_scatter | solution.py:247
  461.3 96.3 %reduce-scatter.13.cloned.1.call-start = ((), (), s32[]{:S(2)}) async-start(), calls=%async_computation.15 | async-start | bytes 1474560 | tf_op jit(solution)/shard_map/reduce_scatter | solution.py:282
  463.8 153.7 %reduce-scatter.17.cloned.1.call-start = ((), (), s32[]{:S(2)}) async-start(), calls=%async_computation.17 | async-start | bytes 5898240 | tf_op jit(solution)/shard_map/reduce_scatter | solution.py:179
  467.9 209.8 %reduce-scatter.15.cloned.1.call-start = ((), (), s32[]{:S(2)}) async-start(), calls=%async_computation.16 | async-start | bytes 5898240 | tf_op jit(solution)/shard_map/reduce_scatter | solution.py:173
  472.9 55.9 %copy-start.5 = (bf16[128,768]{1,0:T(8,128)(2,1)S(1)}, bf16[128,768]{1,0:T(8,128)(2,1)}, u32[]{:S(2)}) copy-start(bf16[128,768]{1,0:T(8,128)(2,1)} %copy-done.4) | copy-start | bytes 589828
  472.9 55.9 %copy-start.9 = (bf16[12,128,64]{1,2,0:T(8,128)(2,1)S(1)}, bf16[12,128,64]{1,2,0:T(8,128)(2,1)}, u32[]{:S(2)}) copy-start(bf16[12,128,64]{1,2,0:T(8,128)(2,1)} %get-tuple-element.260) | copy-start | bytes 589828
  472.9 254.9 %reduce-scatter.11.cloned.1.call-start = ((), (), s32[]{:S(2)}) async-start(), calls=%async_computation.14 | async-start | bytes 4423680 | tf_op jit(solution)/shard_map/reduce_scatter | solution.py:273
  485.8 46.9 %copy-start.12 = (bf16[128,768]{0,1:T(8,128)(2,1)}, bf16[128,768]{0,1:T(8,128)(2,1)S(1)}, u32[]{:S(2)}) copy-start(bf16[128,768]{0,1:T(8,128)(2,1)S(1)} %copy.48) | copy-start | bytes 589828
  532.7 283.7 %all-reduce.23.cloned.1.call-start = ((), (), s32[]{:S(2)}) async-start(), calls=%async_computation.18 | async-start | bytes 7077888 | tf_op jit(solution)/shard_map/psum | solution.py:292
  534.9 193.0 %copy-start.21 = (bf16[768]{0:T(1024)(128)(2,1)}, bf16[768]{0:T(1024)(128)(2,1)S(1)}, u32[]{:S(2)}) copy-start(bf16[768]{0:T(1024)(128)(2,1)S(1)} %dynamic-update-slice.7) | copy-start | bytes 4612
  728.8 4.3 copy-start.19
  728.8 4.3 copy-start.20
  816.4 4.4 copy-start.11
  (21 other events, 49.8 us)
Sparse Core Ops, SparseCore 0:
  10.0 50.0 all-gather.7
  61.9 57.0 all-gather.17
  121.2 25.0 all-gather.9
  148.3 24.5 all-gather.11
  174.6 27.2 all-gather.13
  203.6 57.2 all-gather.15
  444.3 40.2 reduce-scatter.6
  486.9 39.4 reduce-scatter.8
  529.9 27.6 reduce-scatter.12
  560.4 57.0 reduce-scatter.16
  620.5 57.0 reduce-scatter.14
  680.6 47.2 reduce-scatter.10
  730.5 85.8 all-reduce.22
where the time goes:
time: 837 us; the launch traced here: 831 us
  waiting for transfers between devices  429 us (51%)
  matrix products  171 us (20%)
  local copies, waits for them, and re-layouts  89.3 us (11%)
  blocking collectives  57.3 us (7%)
  loops' own time  39.8 us (5%)
  other arithmetic  25 us (3%)
  between operations  17.7 us (2%)
    reduce_scatter x1, waiting for transfers between devices, body(): lax.psum_scatter(g_wup.astype(jnp.bfloat16), 'fsdp', scatter_dimension=0,...  60.1 us
    reduce_scatter x1, waiting for transfers between devices, body(): lax.psum_scatter(g_wdown.astype(jnp.bfloat16), 'fsdp', scatter_dimension=...  59.9 us
    reduce_scatter x1, waiting for transfers between devices, body(): lax.psum_scatter(g_wqkv.astype(jnp.bfloat16), 'fsdp', scatter_dimension=0...  50.2 us
    all_gather x1, waiting for transfers between devices, body(): lax.all_gather(w_down, 'fsdp', axis=0, tiled=True)  43 us
    psum x1, waiting for transfers between devices, body(): lax.psum(attn_shards[2].astype(jnp.bfloat16), 'ctx').astype(jnp.float32)  40.7 us
    reduce_scatter x1, waiting for transfers between devices, body(): lax.psum_scatter(d_values_all, 'ctx', scatter_dimension=1, tiled=True)  40.6 us
    unnamed x2, blocking collectives  33.9 us
    dot_general x24, matrix products, scores_of(): lax.dot_general(qpart, kpart, (((1,), (1,)), ((), ())), preferred_element...  33.1 us
  transfers between devices with their start and end apart: 13, of which 12 were waited for; matrix products, arithmetic and copies ran while one was open for 15% of the time, Pallas kernels for 0%

commit v1 on v0

v1 whole, which is shorter than its diff:
```python
import functools

import jax
import jax.numpy as jnp
from jax import lax
from jax.experimental import pallas as pl
from jax.experimental.pallas import tpu as pltpu
from jax.sharding import PartitionSpec as P

HDIM = 64
EPS = 1e-05
MASKED = -1e30
VMEM_LIMIT = 56 * 1024 * 1024
F32 = jnp.float32
BF16 = jnp.bfloat16


def norm_rows(z, gain, shift):
    mean = jnp.mean(z, axis=-1, keepdims=True)
    cent = z - mean
    var = jnp.mean(cent * cent, axis=-1, keepdims=True)
    return cent * lax.rsqrt(var + EPS) * gain + shift


def mm(a, b, ca, cb):
    return lax.dot_general(a, b, (((ca,), (cb,)), ((), ())), preferred_element_type=F32)


def head_pair(part, scale):
    lane = lax.broadcasted_iota(jnp.int32, part.shape, 1)
    part = (part.astype(F32) * scale).astype(part.dtype)
    zero = jnp.zeros_like(part)
    return jnp.concatenate(
        [jnp.where(lane < HDIM, part, zero), jnp.where(lane < HDIM, zero, part)], axis=0
    )


def join_pair(both):
    rows = both.shape[0] // 2
    lane = lax.broadcasted_iota(jnp.int32, (rows, both.shape[1]), 1)
    return jnp.where(lane < HDIM, both[:rows], both[rows:])


def mask_bias(qpos_ref, kpos_ref):
    seen = qpos_ref[...] >= kpos_ref[...]
    bias = jnp.where(seen, 0.0, MASKED)
    return jnp.concatenate([bias, bias], axis=0)


def attn_fwd_kernel(qkv_ref, kv_ref, qpos_ref, kpos_ref, out_ref, lse_ref, bias_ref):
    width = out_ref.shape[1]
    bias_ref[...] = mask_bias(qpos_ref, kpos_ref)
    for pair in range(width // 128):
        col = pair * 128
        query = head_pair(qkv_ref[:, col : col + 128], HDIM**-0.5)
        scores = mm(query, kv_ref[:, col : col + 128], 1, 1) + bias_ref[...]
        top = jnp.max(scores, axis=1, keepdims=True)
        expo = jnp.exp(scores - top)
        total = jnp.sum(expo, axis=1, keepdims=True)
        res = mm(expo.astype(BF16), kv_ref[:, width + col : width + col + 128], 1, 0)
        out_ref[:, col : col + 128] = join_pair(res / total).astype(BF16)
        lse_ref[:, pair : pair + 1] = top + jnp.log(total)


def attn_bwd_kernel(qkv_ref, kv_ref, do_ref, lse_ref, qpos_ref, kpos_ref, dq_ref, dkv_ref, bias_ref):
    width = dq_ref.shape[1]
    scale = HDIM**-0.5
    bias_ref[...] = mask_bias(qpos_ref, kpos_ref)
    for pair in range(width // 128):
        col = pair * 128
        query = head_pair(qkv_ref[:, col : col + 128], scale)
        d_out = head_pair(do_ref[:, col : col + 128], 1.0)
        keys = kv_ref[:, col : col + 128]
        scores = mm(query, keys, 1, 1) + bias_ref[...]
        probs = jnp.exp(scores - lse_ref[:, pair : pair + 1])
        dkv_ref[:, width + col : width + col + 128] = mm(probs.astype(BF16), d_out, 0, 0).astype(BF16)
        d_probs = mm(d_out, kv_ref[:, width + col : width + col + 128], 1, 1)
        delta = jnp.sum(probs * d_probs, axis=1, keepdims=True)
        d_scores = (probs * (d_probs - delta)).astype(BF16)
        dq_ref[:, col : col + 128] = (join_pair(mm(d_scores, keys, 1, 0)) * scale).astype(BF16)
        dkv_ref[:, col : col + 128] = mm(d_scores, query, 0, 0).astype(BF16)


def attn_fwd(qkv, kv, qpos, kpos):
    rows, width, span = qkv.shape[0], qkv.shape[1] // 3, kv.shape[0]
    return pl.pallas_call(
        attn_fwd_kernel,
        out_shape=(
            jax.ShapeDtypeStruct((rows, width), BF16),
            jax.ShapeDtypeStruct((2 * rows, 128), F32),
        ),
        scratch_shapes=[pltpu.VMEM((2 * rows, span), F32)],
        compiler_params=pltpu.CompilerParams(vmem_limit_bytes=VMEM_LIMIT),
        name="attn_fwd",
    )(qkv, kv, qpos, kpos)


def attn_bwd(qkv, kv, d_out, lse, qpos, kpos):
    rows, width, span = qkv.shape[0], qkv.shape[1] // 3, kv.shape[0]
    return pl.pallas_call(
        attn_bwd_kernel,
        out_shape=(
            jax.ShapeDtypeStruct((rows, width), BF16),
            jax.ShapeDtypeStruct((span, 2 * width), BF16),
        ),
        scratch_shapes=[pltpu.VMEM((2 * rows, span), F32)],
        compiler_params=pltpu.CompilerParams(vmem_limit_bytes=VMEM_LIMIT),
        name="attn_bwd",
    )(qkv, kv, d_out, lse, qpos, kpos)


class PlainComm:

    def gather(self, *arrays):
        return [lax.all_gather(a, "fsdp", axis=0, tiled=True) for a in arrays]

    def gather_attn(self, w_qkv, w_out, small):
        return self.gather(w_qkv, w_out, small[None])

    def gather_mlp(self, qkv, w_up, w_down):
        kv = lax.all_gather(qkv[:, qkv.shape[1] // 3 :], "ctx", axis=0, tiled=True)
        return kv, *self.gather(w_up, w_down)

    def reduce(self, *arrays):
        return [
            lax.psum(lax.psum_scatter(a, "fsdp", scatter_dimension=0, tiled=True), "ctx")
            for a in arrays
        ]

    def reduce_mlp(self, d_kv, g_wup, g_wdown):
        own = lax.psum_scatter(d_kv, "ctx", scatter_dimension=0, tiled=True)
        return own, *self.reduce(g_wup, g_wdown)

    def reduce_attn(self, g_wqkv, g_wout, g_small):
        s_wqkv, s_wout, s_small = self.reduce(g_wqkv, g_wout, g_small)
        return s_wqkv, s_wout, s_small.reshape(-1)


def body(
    tokens, cotangent, pair_of_rank, ln1_gain, ln1_shift, w_qkv, bias_q, bias_v, w_out, bias_out,
    ln2_gain, ln2_shift, w_up, bias_up, w_down, bias_down, *, comm
):
    blk, width = tokens.shape[3], tokens.shape[4]
    shards = lax.axis_size("fsdp")
    parts = lax.axis_size("ctx")
    rank = lax.axis_index("ctx")
    rows = tokens.shape[0] * 2 * blk
    span = parts * 2 * blk
    ff = w_up.shape[1]
    each = ln1_gain.shape[0]

    small = jnp.concatenate(
        [ln1_gain, ln1_shift, bias_q, bias_v, bias_out, ln2_gain, ln2_shift, bias_down, bias_up]
    )
    wqkv_all, wout_all, small_all = comm.gather_attn(w_qkv, w_out, small)
    small_all = small_all.astype(F32)
    vec = lambda i: small_all[:, i * each : (i + 1) * each].reshape(width)
    gain1, shift1, bq_all, bv_all, bout_all, gain2, shift2, bdown_all = (vec(i) for i in range(8))
    bup_all = small_all[:, 8 * each :].reshape(ff)

    inputs = tokens.reshape(rows, width).astype(F32)
    a_one = norm_rows(inputs, gain1, shift1).astype(BF16)
    qkv_bias = jnp.concatenate([bq_all, jnp.zeros((width,), F32), bv_all])
    qkv = (mm(a_one, wqkv_all, 1, 0) + qkv_bias).astype(BF16)
    kv, wup_all, wdown_all = comm.gather_mlp(qkv, w_up, w_down)

    own = pair_of_rank[rank]
    offsets = jnp.arange(blk, dtype=jnp.int32)
    qpos = jnp.concatenate([own * blk + offsets, (2 * parts - 1 - own) * blk + offsets])[:, None]
    key_blocks = jnp.stack([pair_of_rank, 2 * parts - 1 - pair_of_rank], axis=1)
    kpos = (key_blocks[:, :, None] * blk + offsets[None, None, :]).reshape(1, span)

    mixed, lse = attn_fwd(qkv, kv, qpos, kpos)
    resid = inputs + mm(mixed, wout_all, 1, 0) + bout_all
    a_two = norm_rows(resid, gain2, shift2).astype(BF16)
    upper = mm(a_two, wup_all, 1, 0) + bup_all
    active, gelu_pull = jax.vjp(jax.nn.gelu, upper)
    a_three = active.astype(BF16)
    layer_out = (resid + mm(a_three, wdown_all, 1, 0) + bdown_all).astype(BF16).reshape(tokens.shape)

    d_mlp = cotangent.reshape(rows, width)
    grad_rows = d_mlp.astype(F32)
    g_bdown = jnp.sum(grad_rows, axis=0)
    g_wdown = mm(a_three, d_mlp, 0, 0).astype(BF16)
    d_upper = gelu_pull(mm(d_mlp, wdown_all, 1, 1))[0].astype(BF16)
    g_bup = jnp.sum(d_upper.astype(F32), axis=0)
    g_wup = mm(a_two, d_upper, 0, 0).astype(BF16)
    d_htwo = mm(d_upper, wup_all, 1, 1)
    d_resid_norm, g_gain2, g_shift2 = jax.vjp(norm_rows, resid, gain2, shift2)[1](d_htwo)
    d_resid = grad_rows + d_resid_norm
    d_branch = d_resid.astype(BF16)
    g_bout = jnp.sum(d_branch.astype(F32), axis=0)
    g_wout = mm(mixed, d_branch, 0, 0).astype(BF16)
    d_mixed = mm(d_branch, wout_all, 1, 1).astype(BF16)

    d_query, d_kv_all = attn_bwd(qkv, kv, d_mixed, lse, qpos, kpos)
    d_kv, s_wup, s_wdown = comm.reduce_mlp(d_kv_all, g_wup, g_wdown)
    d_qkv = jnp.concatenate([d_query, d_kv], axis=1)
    g_bq = jnp.sum(d_query.astype(F32), axis=0)
    g_bv = jnp.sum(d_kv[:, width:].astype(F32), axis=0)
    g_wqkv = mm(a_one, d_qkv, 0, 0).astype(BF16)
    d_hone = mm(d_qkv, wqkv_all, 1, 1)
    d_input_norm, g_gain1, g_shift1 = jax.vjp(norm_rows, inputs, gain1, shift1)[1](d_hone)
    grad_tokens = (d_resid + d_input_norm).astype(BF16).reshape(tokens.shape)

    cut = lambda g: g.reshape(shards, -1)
    g_small = jnp.concatenate(
        [cut(g) for g in (g_gain1, g_shift1, g_bq, g_bv, g_bout, g_gain2, g_shift2, g_bdown, g_bup)],
        axis=1,
    ).astype(BF16)
    s_wqkv, s_wout, s_small = comm.reduce_attn(g_wqkv, g_wout, g_small)
    s_small = s_small.astype(F32)
    s_gain1, s_shift1, s_bq, s_bv, s_bout, s_gain2, s_shift2, s_bdown = (
        s_small[i * each : (i + 1) * each] for i in range(8)
    )
    s_bup = s_small[8 * each :]
    return (
        layer_out, grad_tokens, s_gain1, s_shift1, s_wqkv.astype(F32), s_bq, s_bv, s_wout.astype(F32),
        s_bout, s_gain2, s_shift2, s_wup.astype(F32), s_bup, s_wdown.astype(F32), s_bdown,
    )


def solution(mesh):
    split = P("fsdp", "ctx", None, None, None)
    row, mat = P("fsdp"), P("fsdp", None)
    in_specs = (
        split, split, P(), row, row, mat, row, row, mat, row, row, row, mat, row, mat, row,
    )
    out_specs = (
        split, split, row, row, mat, row, row, mat, row, row, row, mat, row, mat, row,
    )
    comm = PlainComm()
    return jax.shard_map(
        functools.partial(body, comm=comm),
        mesh=mesh, in_specs=in_specs, out_specs=out_specs, check_vma=False,
    )
```

time: 837 us -> 612 us (0.73)
  matrix products: 171 us -> 38.6 us
  local copies, waits for them, and re-layouts: 89.3 us -> 17.5 us
  waiting for transfers between devices: 429 us -> 471 us
  loops' own time: 39.8 us -> 0 us
  blocking collectives: 57.3 us -> 40.6 us
  Pallas kernels: 0 us -> 15.6 us
  other arithmetic: 25 us -> 12.1 us
    dot_general x96 -> x12, matrix products: 171 us -> 38.6 us  [mm(): lax.dot_general(a, b, (((ca,), (cb,)), ((), ())), preferred_element_type=...]
    all_gather x6 -> x5, waiting for transfers between devices: 140 us -> 205 us  [the longest x4 170 us: gather(): return [lax.all_gather(a, 'fsdp', axis=0, tiled=True) for a in arrays]]
    another operation x2 -> x0, loops' own time: 39.8 us -> none  [the longest x1 31.5 us: body(): dq_heads, dk_heads, dv_heads = lax.map(backward_head, indices)]
    reshape x6 -> x11, local copies, waits for them, and re-layouts: 35 us -> 4.45 us  [the longest x9 4.29 us: body(): cut = lambda g: g.reshape(shards, -1)]
    reduce_scatter x6 -> x5, waiting for transfers between devices: 245 us -> 218 us  [the longest x4 189 us: reduce(): lax.psum_scatter(a, 'fsdp', scatter_dimension=0, tiled=True)]
    dynamic_slice x24 -> x0, local copies, waits for them, and re-layouts: 21.8 us -> none  [body(): head_outs, log_totals = lax.map(forward_head, indices)]
    unnamed x2 -> x1, blocking collectives: 33.9 us -> 15.2 us
    pallas_call x0 -> x2, Pallas kernels: none -> 15.6 us  [the longest x1 9.76 us: attn_bwd(): pl.pallas_call(attn_bwd_kernel, out_shape=(jax.ShapeDtypeStruct((rows, wi...]
  transfers between devices with their start and end apart: 13 -> 11, of which waited for: 12 -> 11; matrix products, arithmetic and copies ran while one was open for 15% -> 8% of each run, Pallas kernels for 0% -> 1%
where the time goes in v1:
time: 612 us; the launch traced here: 611 us
  waiting for transfers between devices  471 us (77%)
  blocking collectives  40.6 us (7%)
  matrix products  38.6 us (6%)
  local copies, waits for them, and re-layouts  17.5 us (3%)
  between operations  15.7 us (3%)
  Pallas kernels  15.6 us (3%)
  other arithmetic  12.1 us (2%)
    reduce_scatter x4, waiting for transfers between devices, reduce(): lax.psum_scatter(a, 'fsdp', scatter_dimension=0, tiled=True)  189 us
    all_gather x4, waiting for transfers between devices, gather(): return [lax.all_gather(a, 'fsdp', axis=0, tiled=True) for a in arrays]  170 us
    psum x1, waiting for transfers between devices, reduce(): lax.psum(lax.psum_scatter(a, 'fsdp', scatter_dimension=0, tiled=True), 'c...  45.2 us
    dot_general x12, matrix products, mm(): lax.dot_general(a, b, (((ca,), (cb,)), ((), ())), preferred_element_type=...  38.6 us
    all_gather x1, waiting for transfers between devices, gather_mlp(): kv = lax.all_gather(qkv[:, qkv.shape[1] // 3:], 'ctx', axis=0, tiled=True)  35.4 us
    reduce_scatter x1, waiting for transfers between devices, reduce_mlp(): own = lax.psum_scatter(d_kv, 'ctx', scatter_dimension=0, tiled=True)  28.7 us
    psum x1, blocking collectives, reduce(): lax.psum(lax.psum_scatter(a, 'fsdp', scatter_dimension=0, tiled=True), 'c...  15.7 us
    unnamed x1, blocking collectives  15.2 us
  transfers between devices with their start and end apart: 11, of which 11 were waited for; matrix products, arithmetic and copies ran while one was open for 8% of the time, Pallas kernels for 1%

profile of v1, /device:TPU:0, one launch (start us, length us, event | category | flops | bytes accessed | tf_op | source)
XLA Modules:
  0.0 611.4 jit_solution(3028645910122082972)
XLA Ops:
  9.0 9.6 %all-gather.1 = bf16[4,1,2304]{2,1,0:T(2,128)(2,1)S(1)} all-gather(bf16[1,1,2304]{2,1,0:T(2,128)(2,1)S(1)} %reshape.252), channel_id=2, replica_groups=mesh['fsdp'=4,'ctx'=8] {'fsdp'}, dimensions={0}, use_global_device_ids=true | all-gather | bytes 23040 | tf_op jit(solution)/shard_map/all_gather | solution.py:115
  19.8 40.2 %all-gather.8.cloned.1.call-done = bf16[768,2304]{1,0:T(8,128)(2,1)} async-done(((bf16[192,2304]{1,0:T(8,128)(2,1)}), bf16[768,2304]{1,0:T(8,128)(2,1)}) %all-gather.8.cloned.1.call-update) | async-done | bytes 3538960 | tf_op jit(solution)/shard_map/all_gather | solution.py:115
  60.0 2.6 fusion.qkv_ref
  68.5 50.4 %all-gather.16.cloned.1.call-done = bf16[3072,768]{1,0:T(8,128)(2,1)} async-done(((bf16[768,768]{1,0:T(8,128)(2,1)}), bf16[3072,768]{1,0:T(8,128)(2,1)}) %all-gather.16.cloned.1.call-update) | async-done | bytes 4718608 | tf_op jit(solution)/shard_map/all_gather | solution.py:115
  118.9 5.1 fusion.24
  124.0 35.4 %all-gather.10.cloned.1.call-done.kv_ref = bf16[1024,1536]{1,0:T(8,128)(2,1)} async-done(((bf16[128,1536]{1,0:T(8,128)(2,1)}), bf16[1024,1536]{1,0:T(8,128)(2,1)}) %all-gather.10.cloned.1.call-update) | async-done | bytes 3145744 | tf_op jit(solution)/shard_map/all_gather | solution.py:121
  159.4 5.8 attn_fwd.1
  165.3 22.5 %all-gather.12.cloned.1.call-done = bf16[768,768]{1,0:T(8,128)(2,1)} async-done(((bf16[192,768]{1,0:T(8,128)(2,1)}), bf16[768,768]{1,0:T(8,128)(2,1)}) %all-gather.12.cloned.1.call-update) | async-done | bytes 1179664 | tf_op jit(solution)/shard_map/all_gather | solution.py:115
  187.8 1.8 fusion.23
  189.8 56.7 %all-gather.14.cloned.1.call-done = bf16[768,3072]{1,0:T(8,128)(2,1)} async-done(((bf16[192,3072]{1,0:T(8,128)(2,1)}), bf16[768,3072]{1,0:T(8,128)(2,1)}) %all-gather.14.cloned.1.call-update) | async-done | bytes 4718608 | tf_op jit(solution)/shard_map/all_gather | solution.py:115
  246.5 5.6 fusion.15
  252.1 2.3 multiply_reduce_fusion
  257.4 9.8 %attn_bwd.1 = (bf16[128,768]{1,0:T(8,128)(2,1)}, bf16[1024,1536]{1,0:T(8,128)(2,1)}) custom-call(bf16[128,2304]{1,0:T(8,128)(2,1)} %copy-done.3, bf16[1024,1536]{1,0:T(8,128)(2,1)} %all-gather.10.cloned.1.call-done.kv_ref, bf16[128,768]{1,0:T(8,128)(2,1)} %convolution_convert_fusion.4.do_ref, f32[256,128]{1,0:T(8,128)} %get-tuple-element.20.lse_ref, ...), custom_call_target="tpu_custom_call" | custom-call | tf_op jit(solution)/shard_map/attn_bwd/pallas_call | solution.py:100
  268.1 1.5 convolution_convert_fusion.3
  269.7 4.4 convolution_convert_fusion.1
  274.1 3.9 convolution_convert_fusion
  278.9 28.7 %reduce-scatter.6.cloned.1.call-done = bf16[128,1536]{1,0:T(8,128)(2,1)} async-done(((bf16[1024,1536]{1,0:T(8,128)(2,1)}), bf16[128,1536]{1,0:T(8,128)(2,1)}) %reduce-scatter.6.cloned.1.call-update) | async-done | bytes 393232 | tf_op jit(solution)/shard_map/reduce_scatter | solution.py:131
  308.7 2.9 convolution_convert_fusion.2
  315.7 4.3 fusion.10
  320.0 18.8 %reduce-scatter.10.cloned.1.call-done = bf16[192,768]{1,0:T(8,128)(2,1)} async-done(((bf16[768,768]{1,0:T(8,128)(2,1)}), bf16[192,768]{1,0:T(8,128)(2,1)}) %reduce-scatter.10.cloned.1.call-update) | async-done | bytes 294928 | tf_op jit(solution)/shard_map/reduce_scatter | solution.py:126
  338.8 60.1 %reduce-scatter.12.cloned.1.call-done = bf16[192,3072]{1,0:T(8,128)(2,1)} async-done(((bf16[768,3072]{1,0:T(8,128)(2,1)}), bf16[192,3072]{1,0:T(8,128)(2,1)}) %reduce-scatter.12.cloned.1.call-update) | async-done | bytes 1179664 | tf_op jit(solution)/shard_map/reduce_scatter | solution.py:126
  398.9 60.1 %reduce-scatter.14.cloned.1.call-done = bf16[768,768]{1,0:T(8,128)(2,1)} async-done(((bf16[3072,768]{1,0:T(8,128)(2,1)}), bf16[768,768]{1,0:T(8,128)(2,1)}) %reduce-scatter.14.cloned.1.call-update) | async-done | bytes 1179664 | tf_op jit(solution)/shard_map/reduce_scatter | solution.py:126
  459.1 50.2 %reduce-scatter.8.cloned.1.call-done = bf16[192,2304]{1,0:T(8,128)(2,1)} async-done(((bf16[768,2304]{1,0:T(8,128)(2,1)}), bf16[192,2304]{1,0:T(8,128)(2,1)}) %reduce-scatter.8.cloned.1.call-update) | async-done | bytes 884752 | tf_op jit(solution)/shard_map/reduce_scatter | solution.py:126
  509.3 2.0 copy-done
  511.3 3.1 fusion.14
  517.9 15.2 %all-reduce = bf16[4,2304]{1,0:T(4,128)(2,1)S(1)} all-reduce(bf16[4,2304]{1,0:T(4,128)(2,1)S(1)} %concatenate.24), channel_id=4, replica_groups=mesh['fsdp'=4,'ctx'=8] {'fsdp'}, use_global_device_ids=true, to_apply=%region_18.0.clone | all-reduce | flops 9216 | bytes 36864
  533.8 15.7 %psum.35 = bf16[1,2304]{1,0:T(2,128)(2,1)S(1)} all-reduce(bf16[1,2304]{1,0:T(2,128)(2,1)S(1)} %constant_dynamic-slice_fusion), channel_id=1, replica_groups=mesh['fsdp'=4,'ctx'=8] {'ctx'}, use_global_device_ids=true, to_apply=%region_19.0 | all-reduce | flops 2304 | bytes 9216 | tf_op jit(solution)/shard_map/psum | solution.py:126
  550.8 2.2 add_convert_fusion
  553.0 45.2 %all-reduce.4.cloned.1.call-done = (bf16[192,2304]{1,0:T(8,128)(2,1)}, bf16[192,768]{1,0:T(8,128)(2,1)}, bf16[192,3072]{1,0:T(8,128)(2,1)}, bf16[768,768]{1,0:T(8,128)(2,1)}) async-done(((bf16[192,2304]{1,0:T(8,128)(2,1)}, bf16[192,768]{1,0:T(8,128)(2,1)}, bf16[192,3072]{1,0:T(8,128)(2,1)}, bf16[768,768]{1,0:T(8,128)(2,1)}), (bf16[192,2304]{1,0:T(8,128)(2,1)}, bf16[192,768]{1,0:T(8,128)(2,1)}, ...) | async-done | bytes 3538960 | tf_op jit(solution)/shard_map/psum | solution.py:126
  598.2 2.6 convert_element_type.108
  601.6 1.7 convert_element_type.112
  603.3 1.6 convert_element_type.114
  (164 shorter events, 23.8 us)
Async XLA Ops:
  7.3 11.6 %copy-start.1 = (bf16[1,1,2,64,768]{4,3,2,1,0:T(8,128)(2,1)S(1)}, bf16[1,1,2,64,768]{4,3,2,1,0:T(8,128)(2,1)}, u32[]{:S(2)}) copy-start(bf16[1,1,2,64,768]{4,3,2,1,0:T(8,128)(2,1)} %param.16) | copy-start | bytes 589828
  7.3 52.7 %all-gather.8.cloned.1.call-start = ((), (), s32[]{:S(2)}) async-start(), calls=%async_computation.5 | async-start | bytes 4423680 | tf_op jit(solution)/shard_map/all_gather | solution.py:115
  8.0 110.9 %all-gather.16.cloned.1.call-start = ((), (), s32[]{:S(2)}) async-start(), calls=%async_computation.9 | async-start | bytes 5898240 | tf_op jit(solution)/shard_map/all_gather | solution.py:115
  8.8 150.7 %all-gather.10.cloned.1.call-start = ((), (), s32[]{:S(2)}) async-start(), calls=%async_computation.6 | async-start | bytes 3538944 | tf_op jit(solution)/shard_map/all_gather | solution.py:121
  19.1 43.5 %copy-start.16 = (f32[128]{0:T(128)}, f32[128]{0:T(128)S(1)}, u32[]{:S(2)}) copy-start(f32[128]{0:T(128)S(1)} %div.43) | copy-start | bytes 1540
  19.4 43.2 %copy-start.36 = (f32[128]{0:T(128)}, f32[128]{0:T(128)S(1)}, u32[]{:S(2)}) copy-start(f32[128]{0:T(128)S(1)} %add.163) | copy-start | bytes 1540
  19.4 43.2 %copy-start.23 = (f32[128]{0:T(128)}, f32[128]{0:T(128)S(1)}, u32[]{:S(2)}) copy-start(f32[128]{0:T(128)S(1)} %rsqrt.22) | copy-start | bytes 1540
  62.6 61.4 %copy-start.3 = (bf16[128,2304]{1,0:T(8,128)(2,1)}, bf16[128,2304]{1,0:T(8,128)(2,1)S(1)}, u32[]{:S(2)}) copy-start(bf16[128,2304]{1,0:T(8,128)(2,1)S(1)} %fusion.qkv_ref) | copy-start | bytes 1769476
  62.7 56.2 %copy-start.4 = (bf16[1,1,2,64,768]{4,3,2,1,0:T(8,128)(2,1)S(1)}, bf16[1,1,2,64,768]{4,3,2,1,0:T(8,128)(2,1)}, u32[]{:S(2)}) copy-start(bf16[1,1,2,64,768]{4,3,2,1,0:T(8,128)(2,1)} %param.17) | copy-start | bytes 589828
  63.5 124.3 %all-gather.12.cloned.1.call-start = ((), (), s32[]{:S(2)}) async-start(), calls=%async_computation.7 | async-start | bytes 1474560 | tf_op jit(solution)/shard_map/all_gather | solution.py:115
  64.0 182.5 %all-gather.14.cloned.1.call-start = ((), (), s32[]{:S(2)}) async-start(), calls=%async_computation.8 | async-start | bytes 5898240 | tf_op jit(solution)/shard_map/all_gather | solution.py:115
  64.6 243.0 %reduce-scatter.6.cloned.1.call-start = ((), (), s32[]{:S(2)}) async-start(), calls=%async_computation.10 | async-start | bytes 3538944 | tf_op jit(solution)/shard_map/reduce_scatter | solution.py:131
  189.6 64.9 %copy-start.15 = (f32[128]{0:T(128)}, f32[128]{0:T(128)S(1)}, u32[]{:S(2)}) copy-start(f32[128]{0:T(128)S(1)} %broadcast_multiply_fusion.1) | copy-start | bytes 1540
  189.8 64.7 %copy-start.18 = (f32[128]{0:T(128)}, f32[128]{0:T(128)S(1)}, u32[]{:S(2)}) copy-start(f32[128]{0:T(128)S(1)} %fusion.12) | copy-start | bytes 1540
  246.5 5.6 copy-start.6
  254.7 12.5 %copy-start.25 = (f32[128]{0:T(128)}, f32[128]{0:T(128)S(1)}, u32[]{:S(2)}) copy-start(f32[128]{0:T(128)S(1)} %negate_multiply_fusion.1) | copy-start | bytes 1540
  267.2 71.7 %reduce-scatter.10.cloned.1.call-start = ((), (), s32[]{:S(2)}) async-start(), calls=%async_computation.12 | async-start | bytes 1474560 | tf_op jit(solution)/shard_map/reduce_scatter | solution.py:126
  269.6 129.3 %reduce-scatter.12.cloned.1.call-start = ((), (), s32[]{:S(2)}) async-start(), calls=%async_computation.13 | async-start | bytes 5898240 | tf_op jit(solution)/shard_map/reduce_scatter | solution.py:126
  274.0 185.0 %reduce-scatter.14.cloned.1.call-start = ((), (), s32[]{:S(2)}) async-start(), calls=%async_computation.14 | async-start | bytes 5898240 | tf_op jit(solution)/shard_map/reduce_scatter | solution.py:126
  278.0 231.3 %reduce-scatter.8.cloned.1.call-start = ((), (), s32[]{:S(2)}) async-start(), calls=%async_computation.11 | async-start | bytes 4423680 | tf_op jit(solution)/shard_map/reduce_scatter | solution.py:126
  308.7 2.9 copy-start.9
  311.5 2.2 copy-start.21
  311.5 2.8 copy-start.20
  311.5 3.5 copy-start.19
  311.6 4.2 copy-start.22
  311.6 286.6 %all-reduce.4.cloned.1.call-start = ((), (), s32[]{:S(2)}) async-start(), calls=%async_computation.15 | async-start | bytes 7077888 | tf_op jit(solution)/shard_map/psum | solution.py:126
  315.7 193.6 %copy-start.17 = (f32[128]{0:T(128)S(1)}, f32[128]{0:T(128)}, u32[]{:S(2)}) copy-start(f32[128]{0:T(128)} %copy-done.16) | copy-start | bytes 1540
  511.3 3.1 copy-start.37
  511.3 3.1 copy-start.2
  511.3 3.1 copy-start.24
  598.2 2.6 copy-start.13
  598.2 3.5 copy-start.11
  (18 other events, 26.5 us)
Sparse Core Ops, SparseCore 0:
  10.0 49.9 all-gather.7
  61.8 57.0 all-gather.15
  121.1 38.2 all-gather.9
  161.1 26.5 all-gather.11
  189.4 57.0 all-gather.13
  267.3 40.2 reduce-scatter.5
  311.1 27.6 reduce-scatter.9
  341.8 57.0 reduce-scatter.11
  401.9 57.0 reduce-scatter.13
  462.0 47.2 reduce-scatter.7
  511.9 86.1 all-reduce.3

commit v2 on v1

--- a/solution.py
+++ b/solution.py
@@ -13,6 +13,7 @@
 VMEM_LIMIT = 56 * 1024 * 1024
 F32 = jnp.float32
 BF16 = jnp.bfloat16
+MESH = pl.DeviceIdType.MESH
 
 
 def norm_rows(z, gain, shift):
@@ -136,6 +137,382 @@
         return s_wqkv, s_wout, s_small.reshape(-1)
 
 
+class Place:
+
+    def __init__(self):
+        self.f = lax.axis_index("fsdp")
+        self.c = lax.axis_index("ctx")
+        self.nz = lax.axis_size("ctx") // 2
+        self.z = lax.div(self.c, 2)
+        self.core = lax.rem(self.c, 2)
+        self.fx = self.f + 1 - 2 * lax.rem(self.f, 2)
+        self.fy = lax.rem(self.f + 2, 4)
+        self.fd = lax.rem(self.fx + 2, 4)
+        self.x_dev = (self.fx, self.c)
+        self.y_dev = (self.fy, self.c)
+        self.sib_dev = (self.f, self.c + 1 - 2 * self.core)
+
+    def z_ahead(self, k):
+        return lax.rem(self.z + k, self.nz)
+
+    def z_behind(self, k):
+        return lax.rem(self.z + self.nz - k, self.nz)
+
+    def z_dev(self, z):
+        return (self.f, 2 * z + self.core)
+
+    def greet(self, along_z):
+        partners = [self.x_dev, self.y_dev, self.sib_dev]
+        if along_z:
+            partners += [self.z_dev(self.z_ahead(k)) for k in range(1, self.nz)]
+        barrier = pltpu.get_barrier_semaphore()
+        for dev in partners:
+            pl.semaphore_signal(barrier, inc=1, device_id=dev, device_id_type=MESH)
+        pl.semaphore_wait(barrier, len(partners))
+
+
+def at(start, size, unit):
+    return pl.ds(pl.multiple_of(start, unit), size)
+
+
+def send(src, dst, sems, row, idx, dev):
+    copy = pltpu.make_async_remote_copy(
+        src_ref=src, dst_ref=dst, send_sem=sems[0].at[row, idx], recv_sem=sems[1].at[row, idx],
+        device_id=dev, device_id_type=MESH,
+    )
+    copy.start()
+    return copy
+
+
+def gather_kernel(count, with_kv, *refs):
+    place = Place()
+    n_in = count + with_kv
+    shards, outs = refs[:count], refs[n_in : n_in + count]
+    rest = refs[2 * n_in :]
+    sems, local = rest[:2], rest[2]
+    place.greet(with_kv)
+    started, stay = [], []
+
+    def piece(i, src, sub):
+        rows, cols = shards[i].shape
+        half, wide = rows // 2, cols // 2
+        return outs[i].at[at(src * rows + sub * half, half, 16), at(place.core * wide, wide, 128)]
+
+    first, second, third = [], [], []
+    for i in range(count):
+        rows, cols = shards[i].shape
+        half, wide = rows // 2, cols // 2
+        mine = [
+            shards[i].at[pl.ds(sub * half, half), at(place.core * wide, wide, 128)] for sub in (0, 1)
+        ]
+        to = [piece(i, place.f, sub) for sub in (0, 1)]
+        xa = send(mine[0], to[0], sems, i, 0, place.x_dev)
+        yb = send(mine[1], to[1], sems, i, 3, place.y_dev)
+        xb = send(mine[1], to[1], sems, i, 1, place.x_dev)
+        ya = send(mine[0], to[0], sems, i, 2, place.y_dev)
+        first.append((i, xa, yb, xb, ya))
+        own = pltpu.make_async_copy(
+            shards[i], outs[i].at[at(place.f * rows, rows, 16), :], local.at[i]
+        )
+        own.start()
+        stay.append(own)
+
+    if with_kv:
+        qkv, kv_out = refs[count], refs[n_in + count]
+        rows, cols = kv_out.shape[0] // (2 * place.nz), kv_out.shape[1]
+        block = qkv.at[:, pl.ds(qkv.shape[1] - cols, cols)]
+        spot = lambda c: kv_out.at[at(c * rows, rows, 16), :]
+        kv_moves = [
+            send(block, spot(place.c), sems, count, k, place.z_dev(place.z_ahead(k)))
+            for k in range(1, place.nz)
+        ]
+        started += [send(block, spot(place.c), sems, count, 0, place.sib_dev)]
+        own = pltpu.make_async_copy(block, spot(place.c), local.at[count])
+        own.start()
+        stay.append(own)
+
+    def pass_on(i, src, sub, idx):
+        ref = piece(i, src, sub)
+        return send(ref, ref, sems, i, idx, place.sib_dev)
+
+    for i, xa, yb, xb, ya in first:
+        xa.wait_recv()
+        ref = piece(i, place.fx, 0)
+        fa = send(ref, ref, sems, i, 4, place.y_dev)
+        yb.wait_recv()
+        ref = piece(i, place.fy, 1)
+        fb = send(ref, ref, sems, i, 5, place.x_dev)
+        second.append((i, fa, fb))
+        started += [pass_on(i, place.fx, 0, 6), pass_on(i, place.fy, 1, 7)]
+        xb.wait_recv()
+        ya.wait_recv()
+        started += [pass_on(i, place.fx, 1, 8), pass_on(i, place.fy, 0, 9)]
+        third += [xa, yb, xb, ya]
+    if with_kv:
+        for k in range(1, place.nz):
+            kv_moves[k - 1].wait_recv()
+            ref = spot(2 * place.z_behind(k) + place.core)
+            started.append(send(ref, ref, sems, count, place.nz + k, place.sib_dev))
+        third += kv_moves
+    for i, fa, fb in second:
+        fa.wait_recv()
+        fb.wait_recv()
+        started += [pass_on(i, place.fd, 0, 10), pass_on(i, place.fd, 1, 11)]
+        third += [fa, fb]
+    for copy in third:
+        copy.wait_send()
+    for copy in started:
+        copy.wait()
+    for copy in stay:
+        copy.wait()
+
+
+def gather_call(arrays, qkv, number):
+    count, with_kv = len(arrays), int(qkv is not None)
+    shards, parts = lax.axis_size("fsdp"), lax.axis_size("ctx")
+    out = [jax.ShapeDtypeStruct((shards * a.shape[0], a.shape[1]), BF16) for a in arrays]
+    args = list(arrays)
+    if with_kv:
+        args.append(qkv)
+        out.append(jax.ShapeDtypeStruct((parts * qkv.shape[0], qkv.shape[1] // 3 * 2), BF16))
+    sems = pltpu.SemaphoreType.DMA((count + with_kv, 12))
+    return pl.pallas_call(
+        functools.partial(gather_kernel, count, with_kv),
+        out_shape=tuple(out),
+        in_specs=[pl.BlockSpec(memory_space=pl.ANY)] * len(args),
+        out_specs=(pl.BlockSpec(memory_space=pl.ANY),) * len(out),
+        scratch_shapes=[sems, sems, pltpu.SemaphoreType.DMA((count + with_kv,))],
+        compiler_params=pltpu.CompilerParams(
+            collective_id=number, has_side_effects=True, vmem_limit_bytes=VMEM_LIMIT
+        ),
+        name="gather_%d" % number,
+    )(*args)
+
+
+def chunk_width(rows, half):
+    for wide in (384, 256, 128):
+        if half % wide == 0 and (rows * wide <= 768 * 384 or wide == 128):
+            return wide
+
+
+def reduce_kernel(count, with_kv, *refs):
+    place = Place()
+    nz = place.nz
+    n_in = count + with_kv
+    grads, outs = refs[:count], refs[n_in : n_in + count]
+    rest = list(refs[2 * n_in :])
+    sems = (rest.pop(0), rest.pop(0))
+    bufs = [[rest.pop(0) for _ in range(7)] for _ in range(count)]
+    place.greet(True)
+    moves, ends = [], []
+    add = lambda *terms: sum(t.astype(F32) for t in terms).astype(BF16)
+
+    jobs = []
+    for i in range(count):
+        rows, half = grads[i].shape[0] // 4, grads[i].shape[1] // 2
+        wide = chunk_width(4 * rows, half)
+        jobs += [(i, off, wide) for off in range(0, half, wide)]
+
+    class Job:
+        pass
+
+    work = []
+    if with_kv:
+        d_kv, kv_out = refs[count], refs[n_in + count]
+        kv_sib, kv_sum, kv_got = rest[:3]
+        kv_sems = (rest[3], rest[4])
+        rows = kv_out.shape[0]
+        block = lambda c: d_kv.at[at(c * rows, rows, 16), :]
+        to_sib = []
+        for k in [*range(1, nz), 0]:
+            dest = place.z_ahead(k)
+            to_sib.append(
+                send(block(2 * dest + 1 - place.core), kv_sib.at[k], kv_sems, 0, k, place.sib_dev)
+            )
+    for row, (i, off, wide) in enumerate(jobs):
+        job = Job()
+        job.row, job.i, job.wide = row, i, wide
+        job.rows, job.half = grads[i].shape[0] // 4, grads[i].shape[1] // 2
+        job.cols = pl.ds(off, wide)
+        job.mine = at(place.core * job.half + off, wide, 128)
+        job.his = at((1 - place.core) * job.half + off, wide, 128)
+        job.g, job.out = grads[i], outs[i]
+        job.sib, job.cs, job.one, job.mid, job.two, job.zs, job.zb = bufs[i]
+        job.m0 = send(job.g.at[:, job.his], job.sib.at[:, job.cols], sems, row, 0, place.sib_dev)
+        moves.append(job.m0)
+        work.append(job)
+    if with_kv:
+        kv_moves = []
+        for k, got in zip([*range(1, nz), 0], to_sib):
+            got.wait_recv()
+            dest = place.z_ahead(k)
+            kv_sum[k] = add(block(2 * dest + place.core)[...], kv_sib[k])
+            if k:
+                kv_moves.append(
+                    send(kv_sum.at[k], kv_got.at[k - 1], kv_sems, 0, nz + k, place.z_dev(dest))
+                )
+        moves += to_sib + kv_moves
+
+    def rows_of(job, who, sub):
+        half = job.rows // 2
+        return at(who * job.rows + sub * half, half, 16)
+
+    def stage_one(job):
+        job.m0.wait_recv()
+        job.cs[:, job.cols] = add(job.g[:, job.mine], job.sib[:, job.cols])
+        cut = lambda who, sub: job.cs.at[rows_of(job, who, sub), job.cols]
+        spot = lambda n: job.one.at[n, :, job.cols]
+        job.m1 = [
+            send(cut(place.fd, 0), spot(1), sems, job.row, 2, place.y_dev),
+            send(cut(place.fd, 1), spot(3), sems, job.row, 4, place.x_dev),
+            send(cut(place.fy, 0), spot(0), sems, job.row, 1, place.y_dev),
+            send(cut(place.fx, 1), spot(2), sems, job.row, 3, place.x_dev),
+        ]
+        moves.extend(job.m1)
+
+    def stage_two(job):
+        for move in job.m1[:2]:
+            move.wait_recv()
+        job.mid[0, :, job.cols] = add(
+            job.cs[rows_of(job, place.fx, 0), job.cols], job.one[1, :, job.cols]
+        )
+        job.mid[1, :, job.cols] = add(
+            job.cs[rows_of(job, place.fy, 1), job.cols], job.one[3, :, job.cols]
+        )
+        job.m2 = [
+            send(
+                job.mid.at[n, :, job.cols], job.two.at[n, :, job.cols], sems, job.row, 5 + n, dev
+            )
+            for n, dev in ((0, place.x_dev), (1, place.y_dev))
+        ]
+        moves.extend(job.m2)
+
+    def stage_three(job):
+        for move in job.m1[2:] + job.m2:
+            move.wait_recv()
+        half, quarter = job.rows // 2, job.rows // nz
+        for n in (0, 1):
+            job.zs[pl.ds(n * half, half), job.cols] = add(
+                job.cs[rows_of(job, place.f, n), job.cols],
+                job.one[2 * n, :, job.cols],
+                job.two[n, :, job.cols],
+            )
+        job.m3 = []
+        for k in range(1, nz):
+            dest = place.z_ahead(k)
+            job.m3.append(
+                send(
+                    job.zs.at[at(dest * quarter, quarter, 16), job.cols],
+                    job.zb.at[k - 1, :, job.cols],
+                    sems, job.row, 6 + k, place.z_dev(dest),
+                )
+            )
+        moves.extend(job.m3)
+
+    def own_rows(job, z):
+        quarter = job.rows // nz
+        return at(z * quarter, quarter, 16)
+
+    def stage_four(job):
+        for move in job.m3:
+            move.wait_recv()
+        mine = own_rows(job, place.z)
+        job.out[mine, job.mine] = add(
+            job.zs[mine, job.cols], *(job.zb[k, :, job.cols] for k in range(nz - 1))
+        )
+        ref = job.out.at[mine, job.mine]
+        job.m4 = [
+            send(ref, ref, sems, job.row, 5 + nz + k, place.z_dev(place.z_ahead(k)))
+            for k in range(1, nz)
+        ]
+        moves.extend(job.m4)
+        ends.append(send(ref, ref, sems, job.row, 5 + 2 * nz, place.sib_dev))
+
+    def stage_five(job):
+        for k, move in enumerate(job.m4, 1):
+            move.wait_recv()
+            ref = job.out.at[own_rows(job, place.z_behind(k)), job.mine]
+            ends.append(send(ref, ref, sems, job.row, 5 + 2 * nz + k, place.sib_dev))
+
+    stages = ((0, stage_one), (2, stage_two), (3, stage_three), (4, stage_four), (5, stage_five))
+    for step in range(len(work) + 5):
+        for lag, stage in stages:
+            if 0 <= step - lag < len(work):
+                stage(work[step - lag])
+    if with_kv:
+        for move in kv_moves:
+            move.wait_recv()
+        kv_out[...] = add(kv_sum[0], *(kv_got[k] for k in range(nz - 1)))
+    for move in moves:
+        move.wait_send()
+    for move in ends:
+        move.wait()
+
+
+def reduce_call(arrays, d_kv, number):
+    count, with_kv = len(arrays), int(d_kv is not None)
+    nz = lax.axis_size("ctx") // 2
+    out = [jax.ShapeDtypeStruct((a.shape[0] // 4, a.shape[1]), BF16) for a in arrays]
+    args, scratch, jobs = list(arrays), [], 0
+    for a in arrays:
+        rows, half = a.shape[0] // 4, a.shape[1] // 2
+        jobs += half // chunk_width(a.shape[0], half)
+        scratch += [
+            pltpu.VMEM(shape, BF16)
+            for shape in (
+                (4 * rows, half), (4 * rows, half), (4, rows // 2, half), (2, rows // 2, half),
+                (2, rows // 2, half), (rows, half), (nz - 1, rows // nz, half),
+            )
+        ]
+    sems = pltpu.SemaphoreType.DMA((jobs, 5 + 3 * nz))
+    scratch = [sems, sems] + scratch
+    if with_kv:
+        args.append(d_kv)
+        rows, cols = d_kv.shape[0] // (2 * nz), d_kv.shape[1]
+        out.append(jax.ShapeDtypeStruct((rows, cols), BF16))
+        kv_sems = pltpu.SemaphoreType.DMA((1, 2 * nz))
+        scratch += [pltpu.VMEM((nz, rows, cols), BF16)] * 2
+        scratch += [pltpu.VMEM((nz - 1, rows, cols), BF16), kv_sems, kv_sems]
+    return pl.pallas_call(
+        functools.partial(reduce_kernel, count, with_kv),
+        out_shape=tuple(out),
+        in_specs=[pl.BlockSpec(memory_space=pltpu.VMEM)] * len(args),
+        out_specs=(pl.BlockSpec(memory_space=pltpu.VMEM),) * len(out),
+        scratch_shapes=scratch,
+        compiler_params=pltpu.CompilerParams(
+            collective_id=number, has_side_effects=True, vmem_limit_bytes=VMEM_LIMIT
+        ),
+        name="reduce_%d" % number,
+    )(*args)
+
+
+class ChipComm:
+
+    def gather_attn(self, w_qkv, w_out, small):
+        size = small.shape[0]
+        packed = jnp.pad(small, (0, 32 * 256 - size)).reshape(32, 256)
+        wqkv_all, wout_all, small_all = gather_call([w_qkv, w_out, packed], None, 1)
+        return wqkv_all, wout_all, small_all.reshape(-1, 32 * 256)[:, :size]
+
+    def gather_mlp(self, qkv, w_up, w_down):
+        wup_all, wdown_all, kv = gather_call([w_up, w_down], qkv, 2)
+        return kv, wup_all, wdown_all
+
+    def reduce_mlp(self, d_kv, g_wup, g_wdown):
+        s_wup, s_wdown, own = reduce_call([g_wup, g_wdown], d_kv, 3)
+        return own, s_wup, s_wdown
+
+    def reduce_attn(self, g_wqkv, g_wout, g_small):
+        size = g_small.shape[1]
+        packed = jnp.pad(g_small, ((0, 0), (0, 64 * 256 - size))).reshape(-1, 256)
+        s_wqkv, s_wout, s_small = reduce_call([g_wqkv, g_wout, packed], None, 4)
+        return s_wqkv, s_wout, s_small.reshape(-1)[:size]
+
+
+def has_chips(mesh):
+    return mesh.shape["fsdp"] == 4 and mesh.shape["ctx"] == 8
+
+
 def body(
     tokens, cotangent, pair_of_rank, ln1_gain, ln1_shift, w_qkv, bias_q, bias_v, w_out, bias_out,
     ln2_gain, ln2_shift, w_up, bias_up, w_down, bias_down, *, comm
@@ -229,7 +606,7 @@
     out_specs = (
         split, split, row, row, mat, row, row, mat, row, row, row, mat, row, mat, row,
     )
-    comm = PlainComm()
+    comm = ChipComm() if has_chips(mesh) else PlainComm()
     return jax.shard_map(
         functools.partial(body, comm=comm),
         mesh=mesh, in_specs=in_specs, out_specs=out_specs, check_vma=False,

time: 612 us -> 357 us (0.58)
  waiting for transfers between devices: 471 us -> 0 us
  Pallas kernels: 15.6 us -> 300 us
  blocking collectives: 40.6 us -> 0 us
  between operations: 15.7 us -> 2.18 us
  matrix products: 38.6 us -> 28.2 us
    pallas_call x0 -> x4, Pallas kernels: none -> 285 us  [the longest x2 155 us: reduce_call(): pl.pallas_call(functools.partial(reduce_kernel, count, with_kv), out_shap...]
    reduce_scatter x5 -> x0, waiting for transfers between devices: 218 us -> none  [the longest x4 189 us: reduce(): lax.psum_scatter(a, 'fsdp', scatter_dimension=0, tiled=True)]
    all_gather x5 -> x0, waiting for transfers between devices: 205 us -> none  [the longest x4 170 us: gather(): return [lax.all_gather(a, 'fsdp', axis=0, tiled=True) for a in arrays]]
    psum x1 -> x0, waiting for transfers between devices: 45.2 us -> none  [reduce(): lax.psum(lax.psum_scatter(a, 'fsdp', scatter_dimension=0, tiled=True), 'c...]
    psum x1 -> x0, blocking collectives: 15.7 us -> none  [reduce(): lax.psum(lax.psum_scatter(a, 'fsdp', scatter_dimension=0, tiled=True), 'c...]
    unnamed x1 -> x0, blocking collectives: 15.2 us -> none
    dot_general x12, matrix products: 38.6 us -> 28.2 us  [mm(): lax.dot_general(a, b, (((ca,), (cb,)), ((), ())), preferred_element_type=...]
    all_gather x1 -> x0, blocking collectives: 9.65 us -> none  [gather(): return [lax.all_gather(a, 'fsdp', axis=0, tiled=True) for a in arrays]]
  transfers between devices with their start and end apart: 11 -> 0, of which waited for: 11 -> 0; matrix products, arithmetic and copies ran while one was open for 8% -> 0% of each run, Pallas kernels for 1% -> 0%
where the time goes in v2:
time: 357 us
  Pallas kernels  300 us (84%)
  matrix products  28.2 us (8%)
  local copies, waits for them, and re-layouts  14.9 us (4%)
  other arithmetic  11 us (3%)
    pallas_call x2, Pallas kernels, reduce_call(): pl.pallas_call(functools.partial(reduce_kernel, count, with_kv), out_shap...  155 us
    pallas_call x2, Pallas kernels, gather_call(): pl.pallas_call(functools.partial(gather_kernel, count, with_kv), out_shap...  130 us
    dot_general x12, matrix products, mm(): lax.dot_general(a, b, (((ca,), (cb,)), ((), ())), preferred_element_type=...  28.2 us
    pallas_call x1, Pallas kernels, attn_bwd(): pl.pallas_call(attn_bwd_kernel, out_shape=(jax.ShapeDtypeStruct((rows, wi...  9.79 us

profile of v2, /device:TPU:0, one launch (start us, length us, event | category | flops | bytes accessed | tf_op | source)
XLA Modules:
  0.0 356.6 jit_solution(6947578502119679106)
XLA Ops:
  0.7 6.1 %concatenate.20 = bf16[2304]{0:T(1024)(128)(2,1)S(1)} concatenate(bf16[192]{0:T(256)(128)(2,1)} %param.19, bf16[192]{0:T(256)(128)(2,1)} %param.20, bf16[192]{0:T(256)(128)(2,1)} %param.22, bf16[192]{0:T(256)(128)(2,1)} %param.23, bf16[192]{0:T(256)(128)(2,1)} %param.25, bf16[192]{0:T(256)(128)(2,1)} %param.26, bf16[192]{0:T(256)(128)(2,1)} %param.27, bf16[192]{0:T(256)(128)(2,1)} %param.31, ...), dimensions={0} | concatenate | bytes 9216 | tf_op jit(solution)/shard_map/concatenate | solution.py:529
  7.4 41.0 %gather_1.1 = (bf16[768,2304]{1,0:T(8,128)(2,1)}, bf16[768,768]{1,0:T(8,128)(2,1)}, bf16[128,256]{1,0:T(8,128)(2,1)}) custom-call(bf16[192,2304]{1,0:T(8,128)(2,1)} %refs_0_.2, bf16[192,768]{1,0:T(8,128)(2,1)} %refs_1_.2, bf16[32,256]{1,0:T(8,128)(2,1)} %reshape.237.refs_2_), custom_call_target="tpu_custom_call" | custom-call | tf_op jit(solution)/shard_map/gather_1/pallas_call | solution.py:279
  48.4 0.9 reshape.238
  50.5 3.5 fusion.refs_2_.qkv_ref
  53.9 88.8 %gather_2.1 = (bf16[768,3072]{1,0:T(8,128)(2,1)}, bf16[3072,768]{1,0:T(8,128)(2,1)}, bf16[1024,1536]{1,0:T(8,128)(2,1)}) custom-call(bf16[192,3072]{1,0:T(8,128)(2,1)} %refs_0_.3, bf16[768,768]{1,0:T(8,128)(2,1)} %refs_1_.3, bf16[128,2304]{1,0:T(8,128)(2,1)} %fusion.refs_2_.qkv_ref), custom_call_target="tpu_custom_call" | custom-call | tf_op jit(solution)/shard_map/gather_2/pallas_call | solution.py:279
  144.7 0.7 copy.32.qpos_ref
  145.6 0.7 add.159.kpos_ref
  146.3 5.9 %attn_fwd.1 = (bf16[128,768]{1,0:T(8,128)(2,1)}, f32[256,128]{1,0:T(8,128)}) custom-call(bf16[128,2304]{1,0:T(8,128)(2,1)} %fusion.refs_2_.qkv_ref, bf16[1024,1536]{1,0:T(8,128)(2,1)} %get-tuple-element.33.kv_ref, s32[128,1]{1,0:T(8,128)} %copy.32.qpos_ref, s32[1,1024]{1,0:T(1,128)} %add.159.kpos_ref), custom_call_target="tpu_custom_call" | custom-call | tf_op jit(solution)/shard_map/attn_fwd/pallas_call | solution.py:87
  152.2 1.3 fusion.21
  154.0 3.4 convolution_add_fusion.1
  157.8 1.8 fusion.10
  159.6 2.0 fusion.22
  161.7 1.8 multiply_reduce_fusion
  163.9 1.2 convolution_convert_fusion.4.do_ref
  165.1 9.8 %attn_bwd.1 = (bf16[128,768]{1,0:T(8,128)(2,1)}, bf16[1024,1536]{1,0:T(8,128)(2,1)}) custom-call(bf16[128,2304]{1,0:T(8,128)(2,1)} %fusion.refs_2_.qkv_ref, bf16[1024,1536]{1,0:T(8,128)(2,1)} %get-tuple-element.33.kv_ref, bf16[128,768]{1,0:T(8,128)(2,1)} %convolution_convert_fusion.4.do_ref, f32[256,128]{1,0:T(8,128)} %get-tuple-element.38.lse_ref, ...), custom_call_target="tpu_custom_call" | custom-call | tf_op jit(solution)/shard_map/attn_bwd/pallas_call | solution.py:101
  174.9 1.0 fusion.18
  175.9 3.6 %convolution_convert_fusion.2.refs_0_ = bf16[768,3072]{1,0:T(8,128)(2,1)} fusion(bf16[128,3072]{1,0:T(8,128)(2,1)S(1)} %get-tuple-element.81, f32[128,768]{1,0:T(8,128)S(1)} %get-tuple-element.77, f32[768]{0:T(1024)S(1)} %add.165, f32[768]{0:T(1024)S(1)} %mul.199, f32[128]{0:T(128)S(1)} %fusion.12, f32[128]{0:T(128)S(1)} %broadcast_multiply_fusion.1), kind=kOutput, calls=%fused_computation.2 | convolution fusion | flops 606830592 | bytes 5905408 | tf_op jit(solution)/shard_map/dot_general | solution.py:27
  179.5 3.8 %convolution_convert_fusion.1.refs_1_ = bf16[3072,768]{1,0:T(8,128)(2,1)} fusion(bf16[128,768]{1,0:T(8,128)(2,1)S(1)} %bitcast.56, f32[128,3072]{1,0:T(8,128)S(1)} %convolution_add_fusion.1), kind=kOutput, calls=%fused_computation.1 | convolution fusion | flops 609878016 | bytes 6488064 | tf_op jit(solution)/shard_map/dot_general | solution.py:27
  183.3 98.1 %reduce_3.1 = (bf16[192,3072]{1,0:T(8,128)(2,1)}, bf16[768,768]{1,0:T(8,128)(2,1)}, bf16[128,1536]{1,0:T(8,128)(2,1)}) custom-call(bf16[768,3072]{1,0:T(8,128)(2,1)} %convolution_convert_fusion.2.refs_0_, bf16[3072,768]{1,0:T(8,128)(2,1)} %convolution_convert_fusion.1.refs_1_, bf16[1024,1536]{1,0:T(8,128)(2,1)} %get-tuple-element.40.refs_2_), custom_call_target="tpu_custom_call" | custom-call | tf_op jit(solution)/shard_map/reduce_3/pallas_call | solution.py:476
  281.4 1.0 constant_dynamic-update-slice_fusion
  282.5 1.4 fusion.14
  284.2 0.9 add_convert_fusion
  285.1 2.9 convolution_convert_fusion.refs_0_
  288.0 1.5 convolution_convert_fusion.3.refs_1_
  290.4 0.7 reshape.253.refs_2_
  291.1 56.8 %reduce_4.1 = (bf16[192,2304]{1,0:T(8,128)(2,1)}, bf16[192,768]{1,0:T(8,128)(2,1)}, bf16[64,256]{1,0:T(8,128)(2,1)}) custom-call(bf16[768,2304]{1,0:T(8,128)(2,1)} %convolution_convert_fusion.refs_0_, bf16[768,768]{1,0:T(8,128)(2,1)} %convolution_convert_fusion.3.refs_1_, bf16[256,256]{1,0:T(8,128)(2,1)} %reshape.253.refs_2_), custom_call_target="tpu_custom_call" | custom-call | tf_op jit(solution)/shard_map/reduce_4/pallas_call | solution.py:476
  347.9 0.7 slice_convert_fusion.1
  348.7 0.7 fusion.20
  349.3 2.6 convert_element_type.118
  351.9 0.9 convert_element_type.119
  352.8 1.7 convert_element_type.120
  355.0 1.6 convert_element_type.121
  (84 shorter events, 5.7 us)
Async XLA Ops:
  0.6 49.0 %copy-start.1 = (bf16[1,1,2,64,768]{4,3,2,1,0:T(8,128)(2,1)S(1)}, bf16[1,1,2,64,768]{4,3,2,1,0:T(8,128)(2,1)}, u32[]{:S(2)}) copy-start(bf16[1,1,2,64,768]{4,3,2,1,0:T(8,128)(2,1)} %param.16) | copy-start | bytes 589828
  53.9 88.8 %copy-start.9 = (s32[8]{0:T(128)S(1)}, s32[8]{0:T(128)}, u32[]{:S(2)}) copy-start(s32[8]{0:T(128)} %param.18) | copy-start | bytes 100
  146.3 5.9 %copy-start.2 = (bf16[768,768]{1,0:T(8,128)(2,1)S(1)}, bf16[768,768]{1,0:T(8,128)(2,1)}, u32[]{:S(2)}) copy-start(bf16[768,768]{1,0:T(8,128)(2,1)} %get-tuple-element.35) | copy-start | bytes 3538948
  154.0 3.8 %copy-start.10 = (bf16[3072,768]{1,0:T(8,128)(2,1)S(1)}, bf16[3072,768]{1,0:T(8,128)(2,1)}, u32[]{:S(2)}) copy-start(bf16[3072,768]{1,0:T(8,128)(2,1)} %get-tuple-element.37) | copy-start | bytes 14155780
  157.8 1.8 copy-start.3
  157.8 3.9 %slice-start = ((s8[4718592]{0:T(1024)(128)(4,1)}), s8[4194304]{0:T(1024)(128)(4,1)S(1)}, s32[]{:S(2)}) async-start(s8[4718592]{0:T(1024)(128)(4,1)} %bitcast.52), calls=%async_computation | async-start | bytes 8388608
  159.6 2.1 slice-start.1
  183.3 99.2 %copy-start = (bf16[768,2304]{1,0:T(8,128)(2,1)S(1)}, bf16[768,2304]{1,0:T(8,128)(2,1)}, u32[]{:S(2)}) copy-start(bf16[768,2304]{1,0:T(8,128)(2,1)} %get-tuple-element.32) | copy-start | bytes 10616836
  285.1 2.9 copy-start.7
  288.0 1.8 copy-start.6
  347.9 4.0 %copy-start.8 = (bf16[192,768]{1,0:T(8,128)(2,1)S(1)}, bf16[192,768]{1,0:T(8,128)(2,1)}, u32[]{:S(2)}) copy-start(bf16[192,768]{1,0:T(8,128)(2,1)} %get-tuple-element.44) | copy-start | bytes 884740
  349.3 3.4 copy-start.5
  352.8 2.3 copy-start.4

commit v3 on v2

--- a/solution.py
+++ b/solution.py
@@ -189,33 +189,32 @@
     n_in = count + with_kv
     shards, outs = refs[:count], refs[n_in : n_in + count]
     rest = refs[2 * n_in :]
-    sems, local = rest[:2], rest[2]
+    sems, local, held = rest[:2], rest[2], rest[3:]
     place.greet(with_kv)
     started, stay = [], []
 
+    def stage_in(i, src, dst):
+        copy = pltpu.make_async_copy(src, held[i], local.at[i, 0])
+        copy.start()
+        stay.append((copy, pltpu.make_async_copy(held[i], dst, local.at[i, 1])))
+
     def piece(i, src, sub):
-        rows, cols = shards[i].shape
-        half, wide = rows // 2, cols // 2
-        return outs[i].at[at(src * rows + sub * half, half, 16), at(place.core * wide, wide, 128)]
+        rows = shards[i].shape[0]
+        part = rows // 4
+        return outs[i].at[at(src * rows + (2 * place.core + sub) * part, part, 16), :]
 
     first, second, third = [], [], []
     for i in range(count):
-        rows, cols = shards[i].shape
-        half, wide = rows // 2, cols // 2
-        mine = [
-            shards[i].at[pl.ds(sub * half, half), at(place.core * wide, wide, 128)] for sub in (0, 1)
-        ]
+        rows = shards[i].shape[0]
+        part = rows // 4
+        mine = [shards[i].at[at((2 * place.core + sub) * part, part, 16), :] for sub in (0, 1)]
         to = [piece(i, place.f, sub) for sub in (0, 1)]
         xa = send(mine[0], to[0], sems, i, 0, place.x_dev)
         yb = send(mine[1], to[1], sems, i, 3, place.y_dev)
         xb = send(mine[1], to[1], sems, i, 1, place.x_dev)
         ya = send(mine[0], to[0], sems, i, 2, place.y_dev)
         first.append((i, xa, yb, xb, ya))
-        own = pltpu.make_async_copy(
-            shards[i], outs[i].at[at(place.f * rows, rows, 16), :], local.at[i]
-        )
-        own.start()
-        stay.append(own)
+        stage_in(i, shards[i], outs[i].at[at(place.f * rows, rows, 16), :])
 
     if with_kv:
         qkv, kv_out = refs[count], refs[n_in + count]
@@ -227,9 +226,11 @@
             for k in range(1, place.nz)
         ]
         started += [send(block, spot(place.c), sems, count, 0, place.sib_dev)]
-        own = pltpu.make_async_copy(block, spot(place.c), local.at[count])
-        own.start()
-        stay.append(own)
+        stage_in(count, block, spot(place.c))
+
+    for copy_in, copy_out in stay:
+        copy_in.wait()
+        copy_out.start()
 
     def pass_on(i, src, sub, idx):
         ref = piece(i, src, sub)
@@ -263,8 +264,8 @@
         copy.wait_send()
     for copy in started:
         copy.wait()
-    for copy in stay:
-        copy.wait()
+    for _, copy_out in stay:
+        copy_out.wait()
 
 
 def gather_call(arrays, qkv, number):
@@ -276,12 +277,15 @@
         args.append(qkv)
         out.append(jax.ShapeDtypeStruct((parts * qkv.shape[0], qkv.shape[1] // 3 * 2), BF16))
     sems = pltpu.SemaphoreType.DMA((count + with_kv, 12))
+    held = [pltpu.VMEM(a.shape, BF16) for a in arrays]
+    if with_kv:
+        held.append(pltpu.VMEM((qkv.shape[0], out[-1].shape[1]), BF16))
     return pl.pallas_call(
         functools.partial(gather_kernel, count, with_kv),
         out_shape=tuple(out),
         in_specs=[pl.BlockSpec(memory_space=pl.ANY)] * len(args),
         out_specs=(pl.BlockSpec(memory_space=pl.ANY),) * len(out),
-        scratch_shapes=[sems, sems, pltpu.SemaphoreType.DMA((count + with_kv,))],
+        scratch_shapes=[sems, sems, pltpu.SemaphoreType.DMA((count + with_kv, 2))] + held,
         compiler_params=pltpu.CompilerParams(
             collective_id=number, has_side_effects=True, vmem_limit_bytes=VMEM_LIMIT
         ),
@@ -490,9 +494,9 @@
 
     def gather_attn(self, w_qkv, w_out, small):
         size = small.shape[0]
-        packed = jnp.pad(small, (0, 32 * 256 - size)).reshape(32, 256)
+        packed = jnp.pad(small, (0, 64 * 128 - size)).reshape(64, 128)
         wqkv_all, wout_all, small_all = gather_call([w_qkv, w_out, packed], None, 1)
-        return wqkv_all, wout_all, small_all.reshape(-1, 32 * 256)[:, :size]
+        return wqkv_all, wout_all, small_all.reshape(-1, 64 * 128)[:, :size]
 
     def gather_mlp(self, qkv, w_up, w_down):
         wup_all, wdown_all, kv = gather_call([w_up, w_down], qkv, 2)

time: 357 us -> 300 us (0.84)
  Pallas kernels: 300 us -> 243 us
    pallas_call x2, Pallas kernels: 130 us -> 72.8 us  [gather_call(): pl.pallas_call(functools.partial(gather_kernel, count, with_kv), out_shap...]
where the time goes in v3:
time: 300 us; the launch traced here: 299 us
  Pallas kernels  243 us (81%)
  matrix products  28.2 us (9%)
  local copies, waits for them, and re-layouts  14.9 us (5%)
  other arithmetic  11 us (4%)
    pallas_call x2, Pallas kernels, reduce_call(): pl.pallas_call(functools.partial(reduce_kernel, count, with_kv), out_shap...  154 us
    pallas_call x2, Pallas kernels, gather_call(): pl.pallas_call(functools.partial(gather_kernel, count, with_kv), out_shap...  72.8 us
    dot_general x12, matrix products, mm(): lax.dot_general(a, b, (((ca,), (cb,)), ((), ())), preferred_element_type=...  28.2 us
    pallas_call x1, Pallas kernels, attn_bwd(): pl.pallas_call(attn_bwd_kernel, out_shape=(jax.ShapeDtypeStruct((rows, wi...  9.76 us
    concatenate x1, local copies, waits for them, and re-layouts, body(): jnp.concatenate([ln1_gain, ln1_shift, bias_q, bias_v, bias_out, ln2_gain,...  6.14 us

profile of v3, /device:TPU:0, one launch (start us, length us, event | category | flops | bytes accessed | tf_op | source)
XLA Modules:
  0.0 299.3 jit_solution(10974271947800811524)
XLA Ops:
  0.7 6.1 %concatenate.20 = bf16[2304]{0:T(1024)(128)(2,1)S(1)} concatenate(bf16[192]{0:T(256)(128)(2,1)} %param.19, bf16[192]{0:T(256)(128)(2,1)} %param.20, bf16[192]{0:T(256)(128)(2,1)} %param.22, bf16[192]{0:T(256)(128)(2,1)} %param.23, bf16[192]{0:T(256)(128)(2,1)} %param.25, bf16[192]{0:T(256)(128)(2,1)} %param.26, bf16[192]{0:T(256)(128)(2,1)} %param.27, bf16[192]{0:T(256)(128)(2,1)} %param.31, ...), dimensions={0} | concatenate | bytes 9216 | tf_op jit(solution)/shard_map/concatenate | solution.py:533
  7.4 26.4 %gather_1.1 = (bf16[768,2304]{1,0:T(8,128)(2,1)}, bf16[768,768]{1,0:T(8,128)(2,1)}, bf16[256,128]{1,0:T(8,128)(2,1)}) custom-call(bf16[192,2304]{1,0:T(8,128)(2,1)} %refs_0_.2, bf16[192,768]{1,0:T(8,128)(2,1)} %refs_1_.2, bf16[64,128]{1,0:T(8,128)(2,1)} %pad_bitcast_fusion.refs_2_), custom_call_target="tpu_custom_call" | custom-call | tf_op jit(solution)/shard_map/gather_1/pallas_call | solution.py:283
  33.8 0.9 reshape.238
  35.9 3.5 %fusion.refs_2_.qkv_ref = bf16[128,2304]{1,0:T(8,128)(2,1)} fusion(bf16[128,768]{1,0:T(8,128)(2,1)S(1)} %add_convert_fusion.2, bf16[768,2304]{1,0:T(8,128)(2,1)} %get-tuple-element.32, f32[2304]{0:T(1024)S(1)} %pad_maximum_fusion), kind=kOutput, calls=%fused_computation.6 | convolution fusion | flops 453574656 | bytes 4334592 | tf_op jit(solution)/shard_map/dot_general | solution.py:27
  39.4 46.4 %gather_2.1 = (bf16[768,3072]{1,0:T(8,128)(2,1)}, bf16[3072,768]{1,0:T(8,128)(2,1)}, bf16[1024,1536]{1,0:T(8,128)(2,1)}) custom-call(bf16[192,3072]{1,0:T(8,128)(2,1)} %refs_0_.3, bf16[768,768]{1,0:T(8,128)(2,1)} %refs_1_.3, bf16[128,2304]{1,0:T(8,128)(2,1)} %fusion.refs_2_.qkv_ref), custom_call_target="tpu_custom_call" | custom-call | tf_op jit(solution)/shard_map/gather_2/pallas_call | solution.py:283
  87.7 0.7 copy.32.qpos_ref
  88.7 0.7 add.159.kpos_ref
  89.3 5.9 %attn_fwd.1 = (bf16[128,768]{1,0:T(8,128)(2,1)}, f32[256,128]{1,0:T(8,128)}) custom-call(bf16[128,2304]{1,0:T(8,128)(2,1)} %fusion.refs_2_.qkv_ref, bf16[1024,1536]{1,0:T(8,128)(2,1)} %get-tuple-element.33.kv_ref, s32[128,1]{1,0:T(8,128)} %copy.32.qpos_ref, s32[1,1024]{1,0:T(1,128)} %add.159.kpos_ref), custom_call_target="tpu_custom_call" | custom-call | tf_op jit(solution)/shard_map/attn_fwd/pallas_call | solution.py:87
  95.3 1.3 fusion.21
  97.1 3.4 %convolution_add_fusion.1 = f32[128,3072]{1,0:T(8,128)S(1)} fusion(bf16[768,3072]{1,0:T(8,128)(2,1)} %get-tuple-element.36, f32[3072]{0:T(1024)S(1)} %add.168, f32[128,768]{1,0:T(8,128)S(1)} %get-tuple-element.77, f32[768]{0:T(1024)S(1)} %add.165, f32[768]{0:T(1024)S(1)} %mul.199, f32[128]{0:T(128)S(1)} %fusion.12, f32[128]{0:T(128)S(1)} %broadcast_multiply_fusion.1), kind=kOutput, calls=%fused_computation.5 | convolution fusion | flops 604864512 | bytes 6704128 | tf_op jit(solution)/shard_map/dot_general | solution.py:27
  100.9 1.8 fusion.10
  102.7 2.0 fusion.22
  104.7 1.8 multiply_reduce_fusion
  107.0 1.2 convolution_convert_fusion.4.do_ref
  108.2 9.8 %attn_bwd.1 = (bf16[128,768]{1,0:T(8,128)(2,1)}, bf16[1024,1536]{1,0:T(8,128)(2,1)}) custom-call(bf16[128,2304]{1,0:T(8,128)(2,1)} %fusion.refs_2_.qkv_ref, bf16[1024,1536]{1,0:T(8,128)(2,1)} %get-tuple-element.33.kv_ref, bf16[128,768]{1,0:T(8,128)(2,1)} %convolution_convert_fusion.4.do_ref, f32[256,128]{1,0:T(8,128)} %get-tuple-element.38.lse_ref, ...), custom_call_target="tpu_custom_call" | custom-call | tf_op jit(solution)/shard_map/attn_bwd/pallas_call | solution.py:101
  117.9 1.0 fusion.18
  118.9 3.6 %convolution_convert_fusion.2.refs_0_ = bf16[768,3072]{1,0:T(8,128)(2,1)} fusion(bf16[128,3072]{1,0:T(8,128)(2,1)S(1)} %get-tuple-element.81, f32[128,768]{1,0:T(8,128)S(1)} %get-tuple-element.77, f32[768]{0:T(1024)S(1)} %add.165, f32[768]{0:T(1024)S(1)} %mul.199, f32[128]{0:T(128)S(1)} %fusion.12, f32[128]{0:T(128)S(1)} %broadcast_multiply_fusion.1), kind=kOutput, calls=%fused_computation.2 | convolution fusion | flops 606830592 | bytes 5905408 | tf_op jit(solution)/shard_map/dot_general | solution.py:27
  122.5 3.8 %convolution_convert_fusion.1.refs_1_ = bf16[3072,768]{1,0:T(8,128)(2,1)} fusion(bf16[128,768]{1,0:T(8,128)(2,1)S(1)} %bitcast.58, f32[128,3072]{1,0:T(8,128)S(1)} %convolution_add_fusion.1), kind=kOutput, calls=%fused_computation.1 | convolution fusion | flops 609878016 | bytes 6488064 | tf_op jit(solution)/shard_map/dot_general | solution.py:27
  126.3 99.9 %reduce_3.1 = (bf16[192,3072]{1,0:T(8,128)(2,1)}, bf16[768,768]{1,0:T(8,128)(2,1)}, bf16[128,1536]{1,0:T(8,128)(2,1)}) custom-call(bf16[768,3072]{1,0:T(8,128)(2,1)} %convolution_convert_fusion.2.refs_0_, bf16[3072,768]{1,0:T(8,128)(2,1)} %convolution_convert_fusion.1.refs_1_, bf16[1024,1536]{1,0:T(8,128)(2,1)} %get-tuple-element.40.refs_2_), custom_call_target="tpu_custom_call" | custom-call | tf_op jit(solution)/shard_map/reduce_3/pallas_call | solution.py:480
  226.2 1.0 constant_dynamic-update-slice_fusion
  227.3 1.4 fusion.14
  229.0 0.9 add_convert_fusion
  229.9 2.9 convolution_convert_fusion.refs_0_
  232.8 1.5 convolution_convert_fusion.3.refs_1_
  235.2 0.7 reshape.253.refs_2_
  235.9 54.6 %reduce_4.1 = (bf16[192,2304]{1,0:T(8,128)(2,1)}, bf16[192,768]{1,0:T(8,128)(2,1)}, bf16[64,256]{1,0:T(8,128)(2,1)}) custom-call(bf16[768,2304]{1,0:T(8,128)(2,1)} %convolution_convert_fusion.refs_0_, bf16[768,768]{1,0:T(8,128)(2,1)} %convolution_convert_fusion.3.refs_1_, bf16[256,256]{1,0:T(8,128)(2,1)} %reshape.253.refs_2_), custom_call_target="tpu_custom_call" | custom-call | tf_op jit(solution)/shard_map/reduce_4/pallas_call | solution.py:480
  290.6 0.7 slice_convert_fusion.1
  291.3 0.7 fusion.20
  292.0 2.6 convert_element_type.118
  294.6 0.9 convert_element_type.119
  295.4 1.7 convert_element_type.120
  297.7 1.6 convert_element_type.121
  (83 shorter events, 5.7 us)
Async XLA Ops:
  0.6 34.4 %copy-start.1 = (bf16[1,1,2,64,768]{4,3,2,1,0:T(8,128)(2,1)S(1)}, bf16[1,1,2,64,768]{4,3,2,1,0:T(8,128)(2,1)}, u32[]{:S(2)}) copy-start(bf16[1,1,2,64,768]{4,3,2,1,0:T(8,128)(2,1)} %param.16) | copy-start | bytes 589828
  39.3 46.4 %copy-start.9 = (s32[8]{0:T(128)S(1)}, s32[8]{0:T(128)}, u32[]{:S(2)}) copy-start(s32[8]{0:T(128)} %param.18) | copy-start | bytes 100
  89.3 5.9 %copy-start.2 = (bf16[768,768]{1,0:T(8,128)(2,1)S(1)}, bf16[768,768]{1,0:T(8,128)(2,1)}, u32[]{:S(2)}) copy-start(bf16[768,768]{1,0:T(8,128)(2,1)} %get-tuple-element.35) | copy-start | bytes 3538948
  97.1 3.8 %copy-start.10 = (bf16[3072,768]{1,0:T(8,128)(2,1)S(1)}, bf16[3072,768]{1,0:T(8,128)(2,1)}, u32[]{:S(2)}) copy-start(bf16[3072,768]{1,0:T(8,128)(2,1)} %get-tuple-element.37) | copy-start | bytes 14155780
  100.9 1.8 copy-start.3
  100.9 3.9 %slice-start = ((s8[4718592]{0:T(1024)(128)(4,1)}), s8[4194304]{0:T(1024)(128)(4,1)S(1)}, s32[]{:S(2)}) async-start(s8[4718592]{0:T(1024)(128)(4,1)} %bitcast.54), calls=%async_computation | async-start | bytes 8388608
  102.7 2.1 slice-start.1
  126.3 100.9 %copy-start = (bf16[768,2304]{1,0:T(8,128)(2,1)S(1)}, bf16[768,2304]{1,0:T(8,128)(2,1)}, u32[]{:S(2)}) copy-start(bf16[768,2304]{1,0:T(8,128)(2,1)} %get-tuple-element.32) | copy-start | bytes 10616836
  229.9 2.9 copy-start.7
  232.8 1.8 copy-start.6
  290.5 4.0 %copy-start.8 = (bf16[192,768]{1,0:T(8,128)(2,1)S(1)}, bf16[192,768]{1,0:T(8,128)(2,1)}, u32[]{:S(2)}) copy-start(bf16[192,768]{1,0:T(8,128)(2,1)} %get-tuple-element.44) | copy-start | bytes 884740
  292.0 3.4 %copy-start.5 = (bf16[192,3072]{1,0:T(8,128)(2,1)S(1)}, bf16[192,3072]{1,0:T(8,128)(2,1)}, u32[]{:S(2)}) copy-start(bf16[192,3072]{1,0:T(8,128)(2,1)} %get-tuple-element.45) | copy-start | bytes 3538948
  295.4 2.3 copy-start.4
